TPU v7x, 32 devices: a whole 2x2x4 slice. The times are simulated.
32 devices in a mesh: cls: 8 (over z, y), dp: 4 (over x, core).
Axes of the slice: x: 2, y: 2, z: 4, core: 2. Of those that a mesh axis runs over, the one named last changes fastest.
Arguments:
- images: bfloat16 [4096, 4096], P(('cls', 'dp')), may hold values from -6 to 6
- defocus: bfloat16 [4096], P(('cls', 'dp')), may hold values from 0.5 to 2
- classes: int32 [4096, 1], P(('cls', 'dp')), may hold values from 0 to 7; in each aligned block of 128 rows (0 to 127, 128 to 255, ...) at most 32 rows name the same one
- rotations: int32 [4096], P(('cls', 'dp')), may hold values from 0 to 63
- references: bfloat16 [8, 64, 4096], P('cls'), may hold values from -6 to 6
Outputs:
- refined: bfloat16 [8, 64, 4096], P('cls', 'dp')
- misfit: float32 [4096], P(('cls', 'dp'))
Inputs may be any that keep to these rules, and one draw needn't show every extreme that they name: `classes`: among the rows of one device no class is named by more than 32 particles, and in every draw some device has exactly 32 particles of one class.
All inputs are finite; a program needn't handle non-finite values.
Results may differ from a plain program's by a relative error of at most 0.008.
Values may be sent and summed in bfloat16 or wider, within the bound.
A program may use at most 64 MiB of HBM per device.

v0:
```python
import jax
import jax.numpy as jnp
from jax import lax
from jax.sharding import PartitionSpec as P

SIDE = 64


def wave_table(side_count):
    pixel_index = jnp.arange(side_count * side_count, dtype=jnp.int32)
    half_side = side_count // 2
    row_freq = (pixel_index // side_count + half_side) % side_count - half_side
    col_freq = (pixel_index % side_count + half_side) % side_count - half_side
    return (row_freq * row_freq + col_freq * col_freq).astype(jnp.float32) / float(
        half_side * half_side
    )


def contrast(defocus_rows, radius):
    phase = 20.0 * defocus_rows.astype(jnp.float32)[:, None] * radius[None, :] + 0.1
    return -jnp.sin(phase) * jnp.exp(-0.5 * radius)[None, :]


def sweep_rows(table, image_rows, rotation_rows, defocus_rows, radius):
    row_total = image_rows.shape[0]
    block_rows = min(64, row_total)
    block_count = row_total // block_rows
    rotation_count = table.shape[0]
    labels = jnp.arange(rotation_count, dtype=jnp.int32)

    def advance(gradient, block_index):
        row_start = block_index * block_rows
        image_block = lax.dynamic_slice_in_dim(image_rows, row_start, block_rows, 0)
        rotation_block = lax.dynamic_slice_in_dim(rotation_rows, row_start, block_rows, 0)
        defocus_block = lax.dynamic_slice_in_dim(defocus_rows, row_start, block_rows, 0)
        selector = (rotation_block[:, None] == labels[None, :]).astype(jnp.bfloat16)
        tiles = jnp.dot(selector, table, preferred_element_type=jnp.float32)
        contrast_rows = contrast(defocus_block, radius)
        residual = contrast_rows * tiles - image_block.astype(jnp.float32)
        misfit_rows = jnp.mean(residual * residual, axis=1)
        weighted = (contrast_rows * residual).astype(jnp.bfloat16)
        gradient = gradient + lax.dot_general(
            selector, weighted, (((0,), (0,)), ((), ())), preferred_element_type=jnp.float32
        )
        return (gradient, misfit_rows)

    start_grad = jnp.zeros((rotation_count, image_rows.shape[1]), jnp.float32)
    gradient, misfit_blocks = lax.scan(
        advance, start_grad, jnp.arange(block_count, dtype=jnp.int32)
    )
    return (gradient, misfit_blocks.reshape(row_total))


def build_slots(
    images, defocus, rotations, class_rows, class_rank, rank_first, slot_width, count_cls
):
    particle_ids = jnp.arange(images.shape[0], dtype=jnp.int32)
    inside = (class_rank >= rank_first) & (class_rank < rank_first + slot_width)
    slot_of = jnp.where(inside, class_rows * slot_width + class_rank - rank_first, -1)
    slot_ids = jnp.arange(count_cls * slot_width, dtype=jnp.int32)
    slot_match = slot_ids[:, None] == slot_of[None, :]
    slot_live = jnp.any(slot_match, axis=1)
    slot_source = jnp.sum(jnp.where(slot_match, particle_ids[None, :], 0), axis=1)
    send_images = jnp.where(
        slot_live[:, None], jnp.take(images, slot_source, axis=0), jnp.zeros((), jnp.bfloat16)
    )
    send_rotation = jnp.where(slot_live, jnp.take(rotations, slot_source), -1)
    send_defocus = jnp.where(
        slot_live, jnp.take(defocus, slot_source).astype(jnp.float32), 0.0
    ).astype(jnp.bfloat16)
    return (send_images, send_rotation, send_defocus)


def shards(images, defocus, classes, rotations, references):
    count_cls = lax.axis_size("cls")
    count_dp = lax.axis_size("dp")
    particle_count = images.shape[0]
    pixel_count = images.shape[1]
    rotation_count = references.shape[1]
    capacity = max(2, 2 * particle_count // count_cls)
    slot_count = count_cls * capacity
    radius = wave_table(SIDE)
    class_rows = classes[:, 0]
    particle_ids = jnp.arange(particle_count, dtype=jnp.int32)
    earlier_same = (class_rows[:, None] == class_rows[None, :]) & (
        particle_ids[None, :] < particle_ids[:, None]
    )
    class_rank = jnp.sum(earlier_same.astype(jnp.int32), axis=1)
    slot_of = class_rows * capacity + class_rank
    slot_ids = jnp.arange(slot_count, dtype=jnp.int32)
    slot_match = slot_ids[:, None] == slot_of[None, :]
    send_images, send_rotation, send_defocus = build_slots(
        images, defocus, rotations, class_rows, class_rank, 0, capacity, count_cls
    )
    recv_images, recv_rotation, recv_defocus = (
        lax.all_to_all(
            send_images.reshape(count_cls, capacity, pixel_count),
            "cls",
            split_axis=0,
            concat_axis=0,
            tiled=True,
        ),
        lax.all_to_all(
            send_rotation.astype(jnp.bfloat16).reshape(count_cls, capacity),
            "cls",
            split_axis=0,
            concat_axis=0,
            tiled=True,
        ),
        lax.all_to_all(
            send_defocus.reshape(count_cls, capacity),
            "cls",
            split_axis=0,
            concat_axis=0,
            tiled=True,
        ),
    )
    image_slots = recv_images.reshape(slot_count, pixel_count)
    rotation_slots = recv_rotation.reshape(slot_count).astype(jnp.int32)
    defocus_slots = recv_defocus.reshape(slot_count)
    labels = jnp.arange(rotation_count, dtype=jnp.int32)
    local_counts = jnp.sum((rotation_slots[:, None] == labels[None, :]).astype(jnp.float32), axis=0)
    counts = lax.psum(local_counts, "dp")
    damping = 0.5 * counts + 1.0
    table = references[0]
    grad_first, unused_first = sweep_rows(table, image_slots, rotation_slots, defocus_slots, radius)
    share_rows = rotation_count // count_dp
    share_start = lax.axis_index("dp") * share_rows
    damping_share = lax.dynamic_slice_in_dim(damping, share_start, share_rows, 0)
    grad_share = lax.psum_scatter(
        grad_first.astype(jnp.bfloat16), "dp", scatter_dimension=0, tiled=True
    ).astype(jnp.float32)
    anchor = lax.dynamic_slice_in_dim(table, share_start, share_rows, 0).astype(jnp.float32)
    fresh_share = (anchor - grad_share / damping_share[:, None]).astype(jnp.bfloat16)
    table_next = lax.all_gather(fresh_share, "dp", axis=0, tiled=True)
    grad_second, misfit_slots = sweep_rows(
        table_next, image_slots, rotation_slots, defocus_slots, radius
    )
    second_share = lax.psum_scatter(
        grad_second.astype(jnp.bfloat16), "dp", scatter_dimension=0, tiled=True
    ).astype(jnp.float32)
    anchor_next = lax.dynamic_slice_in_dim(table_next, share_start, share_rows, 0).astype(
        jnp.float32
    )
    refined = (anchor_next - second_share / damping_share[:, None]).astype(jnp.bfloat16)
    returned = lax.all_to_all(
        misfit_slots.reshape(count_cls, capacity), "cls", split_axis=0, concat_axis=0, tiled=True
    )
    returned_slots = returned.reshape(slot_count)
    misfit = jnp.sum(jnp.where(slot_match, returned_slots[:, None], 0.0), axis=0)
    return (refined.reshape(1, share_rows, pixel_count), misfit)


def solution(mesh):
    in_specs = (
        P(("cls", "dp"), None),
        P(("cls", "dp")),
        P(("cls", "dp"), None),
        P(("cls", "dp")),
        P("cls", None, None),
    )
    out_specs = (P("cls", "dp", None), P(("cls", "dp")))
    return jax.shard_map(shards, mesh=mesh, in_specs=in_specs, out_specs=out_specs, check_vma=False)
```

profile of v0, /device:TPU:0, one launch (start us, length us, event | category | flops | bytes accessed | tf_op | source)
XLA Modules:
  0.0 217.8 jit_solution(12162712561875897432)
XLA Ops:
  7.2 0.9 convert_reduce_fusion.1
  8.1 0.7 multiply_add_fusion.1
  9.1 1.9 gather_fusion.1
  11.2 1.9 gather_fusion
  13.2 0.6 copy.9
  13.8 7.3 %all-to-all-start = ((bf16[8,1,32]{2,1,0:T(2,128)(2,1)}), bf16[8,1,32]{2,1,0:T(2,128)(2,1)S(1)}, u32[]{:S(2)}, u32[]{:S(2)}) async-start(bf16[8,1,32]{2,1,0:T(2,128)(2,1)} %copy.9), calls=%async_computation | async-start | bytes 8192 | tf_op jit(solution)/shard_map/all_to_all | solution.py:103
  21.3 0.6 copy.10
  21.9 1.8 gather_fusion.2
  23.7 3.8 %all-to-all-done = bf16[8,1,32]{2,1,0:T(2,128)(2,1)S(1)} async-done(((bf16[8,1,32]{2,1,0:T(2,128)(2,1)}), bf16[8,1,32]{2,1,0:T(2,128)(2,1)S(1)}, u32[]{:S(2)}, u32[]{:S(2)}) %all-to-all-start) | async-done | bytes 544 | tf_op jit(solution)/shard_map/all_to_all | solution.py:103
  27.5 3.3 %all-to-all-start.1 = ((bf16[8,1,32]{2,1,0:T(2,128)(2,1)}), bf16[8,1,32]{2,1,0:T(2,128)(2,1)S(1)}, u32[]{:S(2)}, u32[]{:S(2)}) async-start(bf16[8,1,32]{2,1,0:T(2,128)(2,1)} %copy.10), calls=%async_computation.1 | async-start | bytes 8192 | tf_op jit(solution)/shard_map/all_to_all | solution.py:110
  30.8 1.6 select_select_fusion
  32.5 4.8 %all-to-all-done.1 = bf16[8,1,32]{2,1,0:T(2,128)(2,1)S(1)} async-done(((bf16[8,1,32]{2,1,0:T(2,128)(2,1)}), bf16[8,1,32]{2,1,0:T(2,128)(2,1)S(1)}, u32[]{:S(2)}, u32[]{:S(2)}) %all-to-all-start.1) | async-done | bytes 544 | tf_op jit(solution)/shard_map/all_to_all | solution.py:110
  37.2 4.3 %all-to-all-start.2 = ((bf16[8,32,4096]{2,1,0:T(8,128)(2,1)}), bf16[8,32,4096]{2,1,0:T(8,128)(2,1)}, u32[]{:S(2)}, u32[]{:S(2)}) async-start(bf16[8,32,4096]{2,1,0:T(8,128)(2,1)} %select_select_fusion), calls=%async_computation.2 | async-start | bytes 4194304 | tf_op jit(solution)/shard_map/all_to_all | solution.py:96
  41.8 45.8 %all-to-all-done.2 = bf16[8,32,4096]{2,1,0:T(8,128)(2,1)} async-done(((bf16[8,32,4096]{2,1,0:T(8,128)(2,1)}), bf16[8,32,4096]{2,1,0:T(8,128)(2,1)}, u32[]{:S(2)}, u32[]{:S(2)}) %all-to-all-start.2) | async-done | bytes 2097184 | tf_op jit(solution)/shard_map/all_to_all | solution.py:96
  87.7 26.6 %while.26 = (s32[]{:T(128)}, f32[64,4096]{1,0:T(8,128)S(1)}, s32[4]{0:T(128)S(1)}, s32[256]{0:T(256)S(1)}, bf16[256]{0:T(256)(128)(2,1)S(1)}, /*index=5*/bf16[64...) while((s32[]{:T(128)}, f32[64,4096]{1,0:T(8,128)S(1)}, ...), condition=%wide.region_4.5_spmd.clone.clone, body=%wide.region_3.4_spmd.clone.clone.sunk | while | flops 70181000 | bytes 3213917 | solution.py:48
  87.7 0.6 dynamic_slice.73
  89.1 5.2 %convolution_add_fusion.4 = f32[64,4096]{1,0:T(8,128)S(1)} fusion(bf16[64,4096]{1,0:T(8,128)(2,1)S(1)} %get-tuple-element.391, f32[64,4096]{1,0:T(8,128)S(1)} %get-tuple-element.374, bf16[256,4096]{1,0:T(8,128)(2,1)} %get-tuple-element.392, s32[]{:T(128)S(6)} %select_n.649, f32[4096]{0:T(1024)S(1)} %get-tuple-element.346, ...), kind=kOutput, calls=%fused_computation.7.clone.1 | convolution fusion | flops 70000640 | bytes 3180037 | tf_op jit(solution)/shard_map/while/body/eval_jaxpr/dot_general | solution.py:42
  94.4 0.6 dynamic_slice.73
  95.8 5.2 %convolution_add_fusion.4 = f32[64,4096]{1,0:T(8,128)S(1)} fusion(bf16[64,4096]{1,0:T(8,128)(2,1)S(1)} %get-tuple-element.391, f32[64,4096]{1,0:T(8,128)S(1)} %get-tuple-element.374, bf16[256,4096]{1,0:T(8,128)(2,1)} %get-tuple-element.392, s32[]{:T(128)S(6)} %select_n.649, f32[4096]{0:T(1024)S(1)} %get-tuple-element.346, ...), kind=kOutput, calls=%fused_computation.7.clone.1 | convolution fusion | flops 70000640 | bytes 3180037 | tf_op jit(solution)/shard_map/while/body/eval_jaxpr/dot_general | solution.py:42
  101.0 0.6 dynamic_slice.73
  102.4 5.2 %convolution_add_fusion.4 = f32[64,4096]{1,0:T(8,128)S(1)} fusion(bf16[64,4096]{1,0:T(8,128)(2,1)S(1)} %get-tuple-element.391, f32[64,4096]{1,0:T(8,128)S(1)} %get-tuple-element.374, bf16[256,4096]{1,0:T(8,128)(2,1)} %get-tuple-element.392, s32[]{:T(128)S(6)} %select_n.649, f32[4096]{0:T(1024)S(1)} %get-tuple-element.346, ...), kind=kOutput, calls=%fused_computation.7.clone.1 | convolution fusion | flops 70000640 | bytes 3180037 | tf_op jit(solution)/shard_map/while/body/eval_jaxpr/dot_general | solution.py:42
  107.7 0.6 dynamic_slice.73
  109.1 5.2 %convolution_add_fusion.4 = f32[64,4096]{1,0:T(8,128)S(1)} fusion(bf16[64,4096]{1,0:T(8,128)(2,1)S(1)} %get-tuple-element.391, f32[64,4096]{1,0:T(8,128)S(1)} %get-tuple-element.374, bf16[256,4096]{1,0:T(8,128)(2,1)} %get-tuple-element.392, s32[]{:T(128)S(6)} %select_n.649, f32[4096]{0:T(1024)S(1)} %get-tuple-element.346, ...), kind=kOutput, calls=%fused_computation.7.clone.1 | convolution fusion | flops 70000640 | bytes 3180037 | tf_op jit(solution)/shard_map/while/body/eval_jaxpr/dot_general | solution.py:42
  114.3 0.9 convert_element_type.114
  115.4 5.7 %psum.7 = f32[64]{0:T(128)S(1)} all-reduce(f32[64]{0:T(128)S(1)} %convert_reduce_fusion), channel_id=1, replica_groups=mesh['cls'=8,'dp'=4] {'dp'}, use_global_device_ids=true, to_apply=%region_7.8 | all-reduce | flops 64 | bytes 512 | tf_op jit(solution)/shard_map/psum | solution.py:123
  121.2 14.7 %reduce-scatter.3.cloned.1.call-done = bf16[16,4096]{1,0:T(8,128)(2,1)} async-done(((bf16[64,4096]{1,0:T(8,128)(2,1)}), bf16[16,4096]{1,0:T(8,128)(2,1)}) %reduce-scatter.3.cloned.1.call-update) | async-done | bytes 131088 | tf_op jit(solution)/shard_map/reduce_scatter | solution.py:130
  135.8 1.0 fusion.68
  136.9 7.4 %all_gather.3 = bf16[64,4096]{1,0:T(8,128)(2,1)} all-gather(bf16[16,4096]{1,0:T(8,128)(2,1)S(1)} %fusion.68), channel_id=1, replica_groups=mesh['cls'=8,'dp'=4] {'dp'}, dimensions={0}, use_global_device_ids=true | all-gather | bytes 655360 | tf_op jit(solution)/shard_map/all_gather | solution.py:135
  144.3 41.9 %while.27 = (s32[]{:T(128)}, f32[64,4096]{1,0:T(8,128)S(1)}, f32[4,64]{1,0:T(4,128)S(1)}, s32[4]{0:T(128)S(1)}, s32[256]{0:T(256)S(1)}, /*index=5*/bf16[256]{0:T...) while((s32[]{:T(128)}, f32[64,4096]{1,0:T(8,128)S(1)}, ...), condition=%wide.region_10.11_spmd.clone.clone, body=%wide.region_8.10_spmd.clone.clone.sunk | while | flops 71753864 | bytes 5344617 | solution.py:48
  144.3 0.6 dynamic_slice.76
  145.7 5.1 %multiply_reduce_fusion.2 = (f32[64]{0:T(128)S(1)}, f32[64,4096]{1,0:T(8,128)S(1)}) fusion(bf16[256,4096]{1,0:T(8,128)(2,1)} %get-tuple-element.434, s32[]{:T(128)S(6)} %select_n.654, bf16[64,4096]{1,0:T(8,128)(2,1)} %get-tuple-element.433, s32[64]{0:T(128)S(1)} %dynamic_slice.77, f32[4096]{0:T(1024)S(1)} %get-tuple-element.356, ...), kind=kOutput, calls=%fused_computation.60.clone.1 | convolution fusion | flops 35917760 | bytes 2130692 | tf_op jit(solution)/shard_map/while/body/eval_jaxpr/dot_general | solution.py:37
  150.8 3.9 %convolution_add_fusion.5 = f32[64,4096]{1,0:T(8,128)S(1)} fusion(f32[64,4096]{1,0:T(8,128)S(1)} %get-tuple-element.414, f32[64,4096]{1,0:T(8,128)S(1)} %get-tuple-element.358, f32[4096]{0:T(1024)S(1)} %get-tuple-element.356, f32[4096]{0:T(1024)S(1)} %get-tuple-element.357, f32[64]{0:T(128)S(1)} %convert_multiply_fusion.5, pred[]{:T(512)S(6)} %compare.12, ...), kind=kOutput, calls=%fused_computation.57.clone.1 | convolution fusion | flops 35655680 | bytes 3179009 | tf_op jit(solution)/shard_map/while/body/eval_jaxpr/dot_general | solution.py:42
  154.7 0.6 dynamic_slice.76
  156.1 5.1 %multiply_reduce_fusion.2 = (f32[64]{0:T(128)S(1)}, f32[64,4096]{1,0:T(8,128)S(1)}) fusion(bf16[256,4096]{1,0:T(8,128)(2,1)} %get-tuple-element.434, s32[]{:T(128)S(6)} %select_n.654, bf16[64,4096]{1,0:T(8,128)(2,1)} %get-tuple-element.433, s32[64]{0:T(128)S(1)} %dynamic_slice.77, f32[4096]{0:T(1024)S(1)} %get-tuple-element.356, ...), kind=kOutput, calls=%fused_computation.60.clone.1 | convolution fusion | flops 35917760 | bytes 2130692 | tf_op jit(solution)/shard_map/while/body/eval_jaxpr/dot_general | solution.py:37
  161.2 3.9 %convolution_add_fusion.5 = f32[64,4096]{1,0:T(8,128)S(1)} fusion(f32[64,4096]{1,0:T(8,128)S(1)} %get-tuple-element.414, f32[64,4096]{1,0:T(8,128)S(1)} %get-tuple-element.358, f32[4096]{0:T(1024)S(1)} %get-tuple-element.356, f32[4096]{0:T(1024)S(1)} %get-tuple-element.357, f32[64]{0:T(128)S(1)} %convert_multiply_fusion.5, pred[]{:T(512)S(6)} %compare.12, ...), kind=kOutput, calls=%fused_computation.57.clone.1 | convolution fusion | flops 35655680 | bytes 3179009 | tf_op jit(solution)/shard_map/while/body/eval_jaxpr/dot_general | solution.py:42
  165.2 0.6 dynamic_slice.76
  166.6 5.1 %multiply_reduce_fusion.2 = (f32[64]{0:T(128)S(1)}, f32[64,4096]{1,0:T(8,128)S(1)}) fusion(bf16[256,4096]{1,0:T(8,128)(2,1)} %get-tuple-element.434, s32[]{:T(128)S(6)} %select_n.654, bf16[64,4096]{1,0:T(8,128)(2,1)} %get-tuple-element.433, s32[64]{0:T(128)S(1)} %dynamic_slice.77, f32[4096]{0:T(1024)S(1)} %get-tuple-element.356, ...), kind=kOutput, calls=%fused_computation.60.clone.1 | convolution fusion | flops 35917760 | bytes 2130692 | tf_op jit(solution)/shard_map/while/body/eval_jaxpr/dot_general | solution.py:37
  171.7 3.9 %convolution_add_fusion.5 = f32[64,4096]{1,0:T(8,128)S(1)} fusion(f32[64,4096]{1,0:T(8,128)S(1)} %get-tuple-element.414, f32[64,4096]{1,0:T(8,128)S(1)} %get-tuple-element.358, f32[4096]{0:T(1024)S(1)} %get-tuple-element.356, f32[4096]{0:T(1024)S(1)} %get-tuple-element.357, f32[64]{0:T(128)S(1)} %convert_multiply_fusion.5, pred[]{:T(512)S(6)} %compare.12, ...), kind=kOutput, calls=%fused_computation.57.clone.1 | convolution fusion | flops 35655680 | bytes 3179009 | tf_op jit(solution)/shard_map/while/body/eval_jaxpr/dot_general | solution.py:42
  175.7 0.6 dynamic_slice.76
  177.1 5.1 %multiply_reduce_fusion.2 = (f32[64]{0:T(128)S(1)}, f32[64,4096]{1,0:T(8,128)S(1)}) fusion(bf16[256,4096]{1,0:T(8,128)(2,1)} %get-tuple-element.434, s32[]{:T(128)S(6)} %select_n.654, bf16[64,4096]{1,0:T(8,128)(2,1)} %get-tuple-element.433, s32[64]{0:T(128)S(1)} %dynamic_slice.77, f32[4096]{0:T(1024)S(1)} %get-tuple-element.356, ...), kind=kOutput, calls=%fused_computation.60.clone.1 | convolution fusion | flops 35917760 | bytes 2130692 | tf_op jit(solution)/shard_map/while/body/eval_jaxpr/dot_general | solution.py:37
  182.2 3.9 %convolution_add_fusion.5 = f32[64,4096]{1,0:T(8,128)S(1)} fusion(f32[64,4096]{1,0:T(8,128)S(1)} %get-tuple-element.414, f32[64,4096]{1,0:T(8,128)S(1)} %get-tuple-element.358, f32[4096]{0:T(1024)S(1)} %get-tuple-element.356, f32[4096]{0:T(1024)S(1)} %get-tuple-element.357, f32[64]{0:T(128)S(1)} %convert_multiply_fusion.5, pred[]{:T(512)S(6)} %compare.12, ...), kind=kOutput, calls=%fused_computation.57.clone.1 | convolution fusion | flops 35655680 | bytes 3179009 | tf_op jit(solution)/shard_map/while/body/eval_jaxpr/dot_general | solution.py:42
  186.1 0.8 convert_element_type.119
  187.1 11.8 %all_to_all.26 = f32[8,1,32]{2,1,0:T(1,128)S(1)} all-to-all(f32[8,1,32]{2,1,0:T(1,128)S(1)} %all_to_all.20), channel_id=1, replica_groups=mesh['cls'=8,'dp'=4] {'cls'}, dimensions={0} | all-to-all | bytes 2048 | tf_op jit(solution)/shard_map/all_to_all | solution.py:146
  198.8 0.5 broadcast.320
  199.4 0.7 reduce.8
  200.1 0.6 select_reduce_fusion
  200.7 8.5 %reduce-scatter.5.cloned.1.call-done = bf16[16,4096]{1,0:T(8,128)(2,1)} async-done(((bf16[64,4096]{1,0:T(8,128)(2,1)}), bf16[16,4096]{1,0:T(8,128)(2,1)}) %reduce-scatter.5.cloned.1.call-update) | async-done | bytes 131088 | tf_op jit(solution)/shard_map/reduce_scatter | solution.py:139
  209.2 1.7 fusion.70
  (67 shorter events, 3.0 us)
Async XLA Ops:
  7.2 14.7 %copy-start = (bf16[128,4096]{1,0:T(8,128)(2,1)S(1)}, bf16[128,4096]{1,0:T(8,128)(2,1)}, u32[]{:S(2)}) copy-start(bf16[128,4096]{1,0:T(8,128)(2,1)} %param.9) | copy-start | bytes 3145732
  13.8 13.7 %all-to-all-start = ((bf16[8,1,32]{2,1,0:T(2,128)(2,1)}), bf16[8,1,32]{2,1,0:T(2,128)(2,1)S(1)}, u32[]{:S(2)}, u32[]{:S(2)}) async-start(bf16[8,1,32]{2,1,0:T(2,128)(2,1)} %copy.9), calls=%async_computation | async-start | bytes 8192 | tf_op jit(solution)/shard_map/all_to_all | solution.py:103
  27.5 9.7 %all-to-all-start.1 = ((bf16[8,1,32]{2,1,0:T(2,128)(2,1)}), bf16[8,1,32]{2,1,0:T(2,128)(2,1)S(1)}, u32[]{:S(2)}, u32[]{:S(2)}) async-start(bf16[8,1,32]{2,1,0:T(2,128)(2,1)} %copy.10), calls=%async_computation.1 | async-start | bytes 8192 | tf_op jit(solution)/shard_map/all_to_all | solution.py:110
  32.5 55.2 %copy-start.1 = (bf16[1,64,4096]{2,1,0:T(8,128)(2,1)S(1)}, bf16[1,64,4096]{2,1,0:T(8,128)(2,1)}, u32[]{:S(2)}) copy-start(bf16[1,64,4096]{2,1,0:T(8,128)(2,1)} %param.13) | copy-start | bytes 1572868
  37.2 50.5 %all-to-all-start.2 = ((bf16[8,32,4096]{2,1,0:T(8,128)(2,1)}), bf16[8,32,4096]{2,1,0:T(8,128)(2,1)}, u32[]{:S(2)}, u32[]{:S(2)}) async-start(bf16[8,32,4096]{2,1,0:T(8,128)(2,1)} %select_select_fusion), calls=%async_computation.2 | async-start | bytes 4194304 | tf_op jit(solution)/shard_map/all_to_all | solution.py:96
  41.6 94.3 %reduce-scatter.3.cloned.1.call-start = ((), (), s32[]{:S(2)}) async-start(), calls=%async_computation.6 | async-start | bytes 655360 | tf_op jit(solution)/shard_map/reduce_scatter | solution.py:130
  115.2 94.0 %reduce-scatter.5.cloned.1.call-start = ((), (), s32[]{:S(2)}) async-start(), calls=%async_computation.7 | async-start | bytes 655360 | tf_op jit(solution)/shard_map/reduce_scatter | solution.py:139
Sparse Core Ops, SparseCore 0:
  115.3 20.4 reduce-scatter.2
  187.1 22.0 reduce-scatter.4
where the time goes:
time: 219 us; the launch traced here: 218 us
  waiting for transfers between devices  77.6 us (35%)
  matrix products  56.8 us (26%)
  blocking collectives  24.8 us (11%)
  starting transfers between devices  15 us (7%)
  between operations  14.2 us (6%)
  local copies, waits for them, and re-layouts  13.7 us (6%)
  other arithmetic  10.2 us (5%)
  loops' own time  5.47 us (2%)
    all_to_all x1, waiting for transfers between devices, shards(): lax.all_to_all(send_images.reshape(count_cls, capacity, pixel_count), 'cl...  45.8 us
    dot_general x8, matrix products, advance(): lax.dot_general(selector, weighted, (((0,), (0,)), ((), ())), preferred_e...  36.5 us
    dot_general x4, matrix products, advance(): tiles = jnp.dot(selector, table, preferred_element_type=jnp.float32)  20.4 us
    reduce_scatter x1, waiting for transfers between devices, shards(): lax.psum_scatter(grad_first.astype(jnp.bfloat16), 'dp', scatter_dimension...  14.7 us
    all_to_all x1, blocking collectives, shards(): lax.all_to_all(misfit_slots.reshape(count_cls, capacity), 'cls', split_ax...  11.8 us
    reduce_scatter x1, waiting for transfers between devices, shards(): lax.psum_scatter(grad_second.astype(jnp.bfloat16), 'dp', scatter_dimensio...  8.48 us
    all_gather x1, blocking collectives, shards(): table_next = lax.all_gather(fresh_share, 'dp', axis=0, tiled=True)  7.4 us
    all_to_all x1, starting transfers between devices, shards(): lax.all_to_all(send_rotation.astype(jnp.bfloat16).reshape(count_cls, capa...  7.28 us
  transfers between devices with their start and end apart: 5, of which 5 were waited for; matrix products, arithmetic and copies ran while one was open for 3% of the time, Pallas kernels for 0%

commit v1 on v0

--- a/solution.py
+++ b/solution.py
@@ -1,9 +1,16 @@
+import functools
 import jax
 import jax.numpy as jnp
+import numpy as np
 from jax import lax
+from jax.experimental import pallas as pl
+from jax.experimental.pallas import tpu as pltpu
 from jax.sharding import PartitionSpec as P
 
 SIDE = 64
+MESH = pl.DeviceIdType.MESH
+CHUNKS = 8
+LANES = 128
 
 
 def wave_table(side_count):
@@ -151,6 +158,435 @@
     return (refined.reshape(1, share_rows, pixel_count), misfit)
 
 
+def radius_tables(side_count):
+    half_side = side_count // 2
+    freq = (np.arange(side_count) + half_side) % side_count - half_side
+    square = (freq[:, None] ** 2 + freq[None, :] ** 2).reshape(-1)
+    values, place = np.unique(square, return_inverse=True)
+    width = -(-(len(values) + 1) // LANES) * LANES
+    rows = np.zeros((8, width), np.float32)
+    rows[0, : len(values)] = values.astype(np.float32) / np.float32(half_side * half_side)
+    rows[1, : len(values)] = -np.exp(-0.5 * rows[0, : len(values)])
+    rows[2, width - 1] = 1.0
+    return rows, place.reshape(1, -1).astype(np.float32)
+
+
+def bounded_sine(angle):
+    turns = jnp.floor(angle * np.float32(1.0 / np.pi) + 0.5)
+    rest = angle - turns * np.float32(3.140625)
+    rest = rest - turns * np.float32(9.67502593994140625e-4)
+    rest = rest - turns * np.float32(1.509957990978376432e-7)
+    odd = turns - 2.0 * jnp.floor(turns * 0.5)
+    sign = 1.0 - 2.0 * odd
+    square = rest * rest
+    poly = np.float32(-2.3889859e-08)
+    poly = poly * square + np.float32(2.7525562e-06)
+    poly = poly * square + np.float32(-1.9840874e-04)
+    poly = poly * square + np.float32(8.3333310e-03)
+    poly = poly * square + np.float32(-1.6666667e-01)
+    return sign * (rest + rest * square * poly)
+
+
+def refine_kernel(
+    sizes,
+    images,
+    meta,
+    tables,
+    place,
+    references,
+    refined,
+    misfit,
+    img,
+    metas,
+    crad,
+    sq,
+    con,
+    pick,
+    hot,
+    hot_t,
+    work,
+    b_own,
+    b_send,
+    y_got,
+    z_own,
+    z_send,
+    z_got,
+    table,
+    s_own,
+    s_send,
+    sy_got,
+    sz_own,
+    sz_send,
+    sz_got,
+    s_sum,
+    anchor,
+    acc,
+    mis,
+    mis_got,
+    send,
+    recv,
+    send_small,
+    recv_small,
+    local,
+):
+    chunks, width, share, side_y, side_z = sizes
+    cls = lax.axis_index("cls")
+    dp = lax.axis_index("dp")
+    z = cls // side_y
+    y = cls % side_y
+    radii = crad.shape[2]
+    half = side_z * share
+    cells = side_y * half
+
+    core_mate = (cls, dp + 1 - 2 * (dp % 2))
+    x_mate = (cls, (dp + 2) % 4)
+    far_mate = (cls, (dp + 2) % 4 + 1 - 2 * (dp % 2))
+    y_mate = (z * side_y + 1 - y, dp)
+    z_mates = [(((z + k) % side_z) * side_y + y, dp) for k in range(1, side_z)]
+
+    barrier = pltpu.get_barrier_semaphore()
+    everyone = [core_mate, x_mate, far_mate, y_mate] + z_mates
+    for other in everyone:
+        pl.semaphore_signal(barrier, inc=1, device_id=other, device_id_type=MESH)
+
+    def remote(source, target, kind, index, device):
+        return pltpu.make_async_remote_copy(
+            src_ref=source,
+            dst_ref=target,
+            send_sem=send.at[kind, index],
+            recv_sem=recv.at[kind, index],
+            device_id=device,
+            device_id_type=MESH,
+        )
+
+    def small(source, target, index, device):
+        return pltpu.make_async_remote_copy(
+            src_ref=source,
+            dst_ref=target,
+            send_sem=send_small.at[index],
+            recv_sem=recv_small.at[index],
+            device_id=device,
+            device_id_type=MESH,
+        )
+
+    def columns(index):
+        return pl.ds(pl.multiple_of(index * width, width), width)
+
+    def own_copy(index):
+        return pltpu.make_async_copy(
+            images.at[:, columns(index)], img.at[0, index], local.at[index]
+        )
+
+    def core_copy(index):
+        return remote(images.at[:, columns(index)], img.at[1, index], 0, index, core_mate)
+
+    def x_copy(index):
+        return remote(images.at[:, columns(index)], img.at[2, index], 1, index, x_mate)
+
+    def forward_copy(index):
+        return remote(img.at[2, index], img.at[3, index], 2, index, core_mate)
+
+    def y_copy(index):
+        return remote(b_send.at[index], y_got.at[index], 3, index, y_mate)
+
+    def z_copy(index, k):
+        return remote(
+            z_send.at[index, k - 1], z_got.at[index, k - 1], 3 + k, index, z_mates[k - 1]
+        )
+
+    def table_z_copy(index, k):
+        rows = pl.ds((side_z - k) * share, share)
+        return remote(
+            table.at[index, pl.ds(0, share)],
+            table.at[index, rows],
+            2 + side_z + k,
+            index,
+            z_mates[k - 1],
+        )
+
+    def table_y_copy(index):
+        return remote(
+            table.at[index, pl.ds(0, half)],
+            table.at[index, pl.ds(half, half)],
+            2 + 2 * side_z,
+            index,
+            y_mate,
+        )
+
+    def meta_copy(k):
+        device = (core_mate, x_mate, far_mate)[k - 1]
+        return small(meta, metas.at[k - 1], k - 1, device)
+
+    def misfit_copy(k):
+        device = (core_mate, x_mate, far_mate)[k - 1]
+        return small(mis.at[k], mis_got.at[k - 1], 2 + k, device)
+
+    s_y_copy = small(s_send, sy_got, 6, y_mate)
+
+    def s_z_copy(k):
+        return small(sz_send.at[k - 1], sz_got.at[k - 1], 6 + k, z_mates[k - 1])
+
+    anchor_copy = pltpu.make_async_copy(
+        references.at[0, pl.ds(pl.multiple_of(dp * share, share), share)],
+        anchor,
+        local.at[chunks],
+    )
+    anchor_copy.start()
+    pl.loop(0, chunks)(lambda index: own_copy(index).start())
+    pl.semaphore_wait(barrier, len(everyone))
+    for k in range(1, 4):
+        meta_copy(k).start()
+
+    @pl.loop(0, chunks)
+    def start_images(index):
+        x_copy(index).start()
+        core_copy(index).start()
+
+    z_first = z.astype(jnp.float32)
+    y_first = y.astype(jnp.float32)
+    r_first = (dp * share).astype(jnp.float32)
+    cell_rows = lax.broadcasted_iota(jnp.int32, (cells, LANES), 0).astype(jnp.float32)
+    cell_lanes = lax.broadcasted_iota(jnp.int32, (LANES, cells), 1).astype(jnp.float32)
+    owned = []
+    for block in range(4):
+        if block > 0:
+            meta_copy(block).wait_recv()
+            rows = metas[block - 1]
+        else:
+            rows = meta[...]
+        class_row = rows[0:1]
+        rel_r = rows[1:2] - r_first
+        class_z = jnp.floor(class_row / float(side_y))
+        rel_y = jnp.abs(class_row - float(side_y) * class_z - y_first)
+        rel_z = class_z - z_first
+        rel_z = jnp.where(rel_z < 0.0, rel_z + float(side_z), rel_z)
+        mine = (rel_r >= 0.0) & (rel_r < float(share))
+        cell = jnp.where(mine, rel_y * float(half) + rel_z * float(share) + rel_r, -1.0)
+        owned.append(mine)
+        hot[:, block * LANES : (block + 1) * LANES] = jnp.where(cell_rows == cell, 1.0, 0.0).astype(
+            jnp.bfloat16
+        )
+        cell_t = jnp.transpose(jnp.broadcast_to(cell, (LANES, LANES)))
+        hot_t[block] = jnp.where(cell_lanes == cell_t, 1.0, 0.0).astype(jnp.bfloat16)
+        focus = jnp.transpose(jnp.broadcast_to(rows[2:3], (LANES, LANES)))
+        for part in range(radii // LANES):
+            lanes = slice(part * LANES, (part + 1) * LANES)
+            phase = 20.0 * focus * tables[0:1, lanes] + 0.1
+            wave = bounded_sine(phase) * tables[1:2, lanes]
+            crad[block, :, lanes] = wave.astype(jnp.bfloat16)
+            sq[block * LANES : (block + 1) * LANES, lanes] = (
+                wave * wave + tables[2:3, lanes]
+            ).astype(jnp.bfloat16)
+    acc[...] = jnp.zeros_like(acc)
+    partial = jnp.dot(hot[...], sq[...], preferred_element_type=jnp.float32)
+    s_own[...] = partial[:half]
+    s_send[...] = partial[half:].astype(jnp.bfloat16)
+    s_y_copy.start()
+
+    def tick(t, carry):
+        @pl.when(t < chunks)
+        def forward():
+            x_copy(t).wait_recv()
+            forward_copy(t).start()
+            target = place[:, columns(t)]
+            index_rows = lax.broadcasted_iota(jnp.int32, (radii, width), 0).astype(jnp.float32)
+            pick[t] = jnp.where(index_rows == target, 1.0, 0.0).astype(jnp.bfloat16)
+            for block in range(4):
+                con[block, t] = jnp.dot(
+                    crad[block], pick[t], preferred_element_type=jnp.float32
+                ).astype(jnp.bfloat16)
+
+        @pl.when(t == 0)
+        def counts_out():
+            s_y_copy.wait_recv()
+            total = s_own[...] + sy_got[...].astype(jnp.float32)
+            sz_own[...] = total[:share]
+            for k in range(1, side_z):
+                sz_send[k - 1] = total[k * share : (k + 1) * share].astype(jnp.bfloat16)
+                s_z_copy(k).start()
+
+        @pl.when((t >= 1) & (t < chunks + 1))
+        def sum_y():
+            index = t - 1
+            y_copy(index).wait_recv()
+            total = b_own[index] + y_got[index].astype(jnp.float32)
+            z_own[index] = total[:share]
+            for k in range(1, side_z):
+                z_send[index, k - 1] = total[k * share : (k + 1) * share].astype(jnp.bfloat16)
+                z_copy(index, k).start()
+
+        @pl.when(t == 2)
+        def counts_in():
+            anchor_copy.wait()
+            total = sz_own[...]
+            for k in range(1, side_z):
+                s_z_copy(k).wait_recv()
+                total = total + sz_got[k - 1].astype(jnp.float32)
+            s_sum[...] = total
+
+        @pl.when((t >= 2) & (t < chunks + 2))
+        def update():
+            index = t - 2
+            total = z_own[index]
+            for k in range(1, side_z):
+                z_copy(index, k).wait_recv()
+                total = total + z_got[index, k - 1].astype(jnp.float32)
+            squares = s_sum[...]
+            coarse = squares.astype(jnp.bfloat16)
+            fine = (squares - coarse.astype(jnp.float32)).astype(jnp.bfloat16)
+            energy = jnp.dot(coarse, pick[index], preferred_element_type=jnp.float32)
+            energy = energy + jnp.dot(fine, pick[index], preferred_element_type=jnp.float32)
+            damping = 0.5 * squares[:, radii - 1 : radii] + 1.0
+            scale = 1.0 / damping
+            start = anchor[:, columns(index)].astype(jnp.float32)
+            first = (start - (start * energy - total) * scale).astype(jnp.bfloat16)
+            table[index, 0:share] = first
+            for k in range(1, side_z):
+                table_z_copy(index, k).start()
+            again = first.astype(jnp.float32)
+            refined[:, columns(index)] = (again - (again * energy - total) * scale).astype(
+                jnp.bfloat16
+            )
+
+        @pl.when((t >= 3) & (t < chunks + 3))
+        def spread():
+            index = t - 3
+            for k in range(1, side_z):
+                table_z_copy(index, k).wait_recv()
+            table_y_copy(index).start()
+
+        @pl.when(t < chunks)
+        def partial_sums():
+            own_copy(t).wait()
+            core_copy(t).wait_recv()
+            forward_copy(t).wait_recv()
+            for block in range(4):
+                work[block * LANES : (block + 1) * LANES] = con[block, t] * img[block, t]
+            total = jnp.dot(hot[...], work[...], preferred_element_type=jnp.float32)
+            b_own[t] = total[:half]
+            b_send[t] = total[half:].astype(jnp.bfloat16)
+            y_copy(t).start()
+
+        @pl.when(t >= 4)
+        def residuals():
+            index = t - 4
+            table_y_copy(index).wait_recv()
+            for block in range(4):
+                tiles = jnp.dot(hot_t[block], table[index], preferred_element_type=jnp.float32)
+                rest = con[block, index].astype(jnp.float32) * tiles - img[block, index].astype(
+                    jnp.float32
+                )
+                rest = rest * rest
+                total = acc[block]
+                for part in range(width // LANES):
+                    total = total + rest[:, part * LANES : (part + 1) * LANES]
+                acc[block] = total
+
+        return carry
+
+    lax.fori_loop(0, chunks + 4, tick, 0)
+
+    for block in (1, 2, 3, 0):
+        row = jnp.sum(jnp.transpose(acc[block]), axis=0, keepdims=True)
+        row = jnp.where(owned[block], row * (1.0 / float(chunks * width)), 0.0)
+        mis[block] = jnp.broadcast_to(row, mis.shape[1:])
+        if block > 0:
+            misfit_copy(block).start()
+
+    @pl.loop(0, chunks)
+    def drain(index):
+        core_copy(index).wait_send()
+        x_copy(index).wait_send()
+        forward_copy(index).wait_send()
+        y_copy(index).wait_send()
+        for k in range(1, side_z):
+            z_copy(index, k).wait_send()
+            table_z_copy(index, k).wait_send()
+        table_y_copy(index).wait_send()
+
+    s_y_copy.wait_send()
+    for k in range(1, side_z):
+        s_z_copy(k).wait_send()
+    total = mis[0]
+    for k in range(1, 4):
+        meta_copy(k).wait_send()
+        misfit_copy(k).wait()
+        total = total + mis_got[k - 1]
+    misfit[...] = total
+
+
+def shards_close(side_y, side_z, images, defocus, classes, rotations, references):
+    count_dp = lax.axis_size("dp")
+    rows, pixels = images.shape
+    share = references.shape[1] // count_dp
+    chunks = CHUNKS
+    width = pixels // chunks
+    half = side_z * share
+    cells = side_y * half
+    tables, place = radius_tables(SIDE)
+    radii = tables.shape[1]
+    meta = jnp.concatenate(
+        [
+            classes.reshape(1, rows).astype(jnp.float32),
+            rotations.reshape(1, rows).astype(jnp.float32),
+            defocus.reshape(1, rows).astype(jnp.float32),
+            jnp.zeros((5, rows), jnp.float32),
+        ],
+        axis=0,
+    )
+    bf16, f32 = jnp.bfloat16, jnp.float32
+    kinds = 3 + 2 * side_z
+    vmem = pl.BlockSpec(memory_space=pltpu.VMEM)
+    anywhere = pl.BlockSpec(memory_space=pl.ANY)
+    refined, misfit = pl.pallas_call(
+        functools.partial(refine_kernel, (chunks, width, share, side_y, side_z)),
+        out_shape=(
+            jax.ShapeDtypeStruct((share, pixels), bf16),
+            jax.ShapeDtypeStruct((8, rows), f32),
+        ),
+        in_specs=[anywhere, vmem, vmem, vmem, anywhere],
+        out_specs=(vmem, vmem),
+        scratch_shapes=[
+            pltpu.VMEM((4, chunks, rows, width), bf16),
+            pltpu.VMEM((3, 8, rows), f32),
+            pltpu.VMEM((4, rows, radii), bf16),
+            pltpu.VMEM((4 * rows, radii), bf16),
+            pltpu.VMEM((4, chunks, rows, width), bf16),
+            pltpu.VMEM((chunks, radii, width), bf16),
+            pltpu.VMEM((cells, 4 * rows), bf16),
+            pltpu.VMEM((4, rows, cells), bf16),
+            pltpu.VMEM((4 * rows, width), bf16),
+            pltpu.VMEM((chunks, half, width), f32),
+            pltpu.VMEM((chunks, half, width), bf16),
+            pltpu.VMEM((chunks, half, width), bf16),
+            pltpu.VMEM((chunks, share, width), f32),
+            pltpu.VMEM((chunks, side_z - 1, share, width), bf16),
+            pltpu.VMEM((chunks, side_z - 1, share, width), bf16),
+            pltpu.VMEM((chunks, cells, width), bf16),
+            pltpu.VMEM((half, radii), f32),
+            pltpu.VMEM((half, radii), bf16),
+            pltpu.VMEM((half, radii), bf16),
+            pltpu.VMEM((share, radii), f32),
+            pltpu.VMEM((side_z - 1, share, radii), bf16),
+            pltpu.VMEM((side_z - 1, share, radii), bf16),
+            pltpu.VMEM((share, radii), f32),
+            pltpu.VMEM((share, pixels), bf16),
+            pltpu.VMEM((4, rows, LANES), f32),
+            pltpu.VMEM((4, 8, rows), f32),
+            pltpu.VMEM((3, 8, rows), f32),
+            pltpu.SemaphoreType.DMA((kinds, chunks)),
+            pltpu.SemaphoreType.DMA((kinds, chunks)),
+            pltpu.SemaphoreType.DMA((6 + side_z,)),
+            pltpu.SemaphoreType.DMA((6 + side_z,)),
+            pltpu.SemaphoreType.DMA((chunks + 1,)),
+        ],
+        compiler_params=pltpu.CompilerParams(
+            collective_id=0, has_side_effects=True, vmem_limit_bytes=48 * 1024 * 1024
+        ),
+    )(images, meta, jnp.asarray(tables), jnp.asarray(place), references)
+    return refined.reshape(1, share, pixels), misfit[0]
+
+
 def solution(mesh):
     in_specs = (
         P(("cls", "dp"), None),
@@ -160,4 +596,9 @@
         P("cls", None, None),
     )
     out_specs = (P("cls", "dp", None), P(("cls", "dp")))
-    return jax.shard_map(shards, mesh=mesh, in_specs=in_specs, out_specs=out_specs, check_vma=False)
+    per_device = shards
+    if mesh.shape["cls"] == 8 and mesh.shape["dp"] == 4:
+        per_device = functools.partial(shards_close, 2, 4)
+    return jax.shard_map(
+        per_device, mesh=mesh, in_specs=in_specs, out_specs=out_specs, check_vma=False
+    )

time: 219 us -> 71.4 us (0.33)
  waiting for transfers between devices: 77.6 us -> 0 us
  Pallas kernels: 0 us -> 64.2 us
  matrix products: 56.8 us -> 0 us
  blocking collectives: 24.8 us -> 0 us
  starting transfers between devices: 15 us -> 0 us
  between operations: 14.2 us -> 0.65 us
  local copies, waits for them, and re-layouts: 13.7 us -> 4.24 us
  other arithmetic: 10.2 us -> 2.05 us
  loops' own time: 5.47 us -> 0 us
    pallas_call x0 -> x1, Pallas kernels: none -> 64.2 us  [shards_close(): pl.pallas_call(functools.partial(refine_kernel, (chunks, width, share, si...]
    dot_general x12 -> x0, matrix products: 56.8 us -> none  [the longest x8 36.5 us: advance(): lax.dot_general(selector, weighted, (((0,), (0,)), ((), ())), preferred_e...]
    all_to_all x3 -> x0, waiting for transfers between devices: 54.4 us -> none  [the longest x1 45.8 us: shards(): lax.all_to_all(send_images.reshape(count_cls, capacity, pixel_count), 'cl...]
    reduce_scatter x2 -> x0, waiting for transfers between devices: 23.2 us -> none  [the longest x1 14.7 us: shards(): lax.psum_scatter(grad_first.astype(jnp.bfloat16), 'dp', scatter_dimension...]
    all_to_all x3 -> x0, starting transfers between devices: 15 us -> none  [the longest x1 7.28 us: shards(): lax.all_to_all(send_rotation.astype(jnp.bfloat16).reshape(count_cls, capa...]
    all_to_all x1 -> x0, blocking collectives: 11.8 us -> none  [shards(): lax.all_to_all(misfit_slots.reshape(count_cls, capacity), 'cls', split_ax...]
    all_gather x1 -> x0, blocking collectives: 7.4 us -> none  [shards(): table_next = lax.all_gather(fresh_share, 'dp', axis=0, tiled=True)]
    gather x5 -> x0, local copies, waits for them, and re-layouts: 5.82 us -> none  [the longest x2 2 us: build_slots(): jnp.take(defocus, slot_source).astype(jnp.float32)]
  transfers between devices with their start and end apart: 5 -> 0, of which waited for: 5 -> 0; matrix products, arithmetic and copies ran while one was open for 3% -> 0% of each run, Pallas kernels for 0% -> 0%
where the time goes in v1:
time: 71.4 us; the launch traced here: 71.1 us
  Pallas kernels  64.2 us (90%)
  local copies, waits for them, and re-layouts  4.24 us (6%)
  other arithmetic  2.05 us (3%)
    pallas_call x1, Pallas kernels, shards_close(): pl.pallas_call(functools.partial(refine_kernel, (chunks, width, share, si...  64.2 us
    unnamed x9, local copies, waits for them, and re-layouts  3.64 us

profile of v1, /device:TPU:0, one launch (start us, length us, event | category | flops | bytes accessed | tf_op | source)
XLA Modules:
  0.0 71.1 jit_solution(11646064354106641863)
XLA Ops:
  0.6 0.0 copy-start.2
  0.6 0.7 bitcast_convert_fusion
  1.3 0.7 convert_bitcast_fusion.1
  2.0 0.7 convert_bitcast_fusion
  2.6 0.1 pad.3.clone
  2.7 0.1 maximum_maximum_fusion.meta
  2.8 0.0 copy-done.2
  2.8 0.0 copy-start
  2.8 1.2 %copy-done = bf16[128,4096]{1,0:T(8,128)(2,1)S(1)} copy-done((bf16[128,4096]{1,0:T(8,128)(2,1)S(1)}, bf16[128,4096]{1,0:T(8,128)(2,1)}, u32[]{:S(2)}) %copy-start) | copy-done | bytes 1048600
  4.0 0.0 copy-start.1
  4.0 1.0 %copy-done.1 = bf16[1,64,4096]{2,1,0:T(8,128)(2,1)S(1)} copy-done((bf16[1,64,4096]{2,1,0:T(8,128)(2,1)S(1)}, bf16[1,64,4096]{2,1,0:T(8,128)(2,1)}, u32[]{:S(2)}) %copy-start.1) | copy-done | bytes 524312
  5.0 0.0 copy-start.3
  5.0 0.7 %copy-done.3 = f32[8,512]{1,0:T(8,128)S(1)} copy-done((f32[8,512]{1,0:T(8,128)S(1)}, f32[8,512]{1,0:T(8,128)}, u32[]{:S(2)}) %copy-start.3) | copy-done | bytes 16408
  5.8 64.2 %shard_map.86 = (bf16[16,4096]{1,0:T(8,128)(2,1)S(1)}, f32[8,128]{1,0:T(8,128)S(1)}) custom-call(bf16[128,4096]{1,0:T(8,128)(2,1)S(1)} %copy-done, f32[8,128]{1,0:T(8,128)S(1)} %maximum_maximum_fusion.meta, f32[8,512]{1,0:T(8,128)S(1)} %copy-done.3, f32[1,4096]{1,0:T(1,128)S(1)} %copy-done.2, bf16[1,64,4096]{2,1,0:T(8,128)(2,1)S(1)} %copy-done.1), custom_call_target="tpu_custom_call" | custom-call | tf_op jit(solution)/shard_map/pallas_call | solution.py:541
  69.9 0.5 slice_bitcast_fusion
  70.4 0.7 copy.10
  (1 shorter events, 0.0 us)
Async XLA Ops:
  0.6 2.1 %copy-start.2 = (f32[1,4096]{1,0:T(1,128)S(1)}, f32[1,4096]{1,0:T(1,128)}, u32[]{:S(2)}) copy-start(f32[1,4096]{1,0:T(1,128)} %constant.7.clone.place) | copy-start | bytes 49156
  2.8 1.2 %copy-start = (bf16[128,4096]{1,0:T(8,128)(2,1)S(1)}, bf16[128,4096]{1,0:T(8,128)(2,1)}, u32[]{:S(2)}) copy-start(bf16[128,4096]{1,0:T(8,128)(2,1)} %images.1) | copy-start | bytes 3145732
  4.0 1.0 %copy-start.1 = (bf16[1,64,4096]{2,1,0:T(8,128)(2,1)S(1)}, bf16[1,64,4096]{2,1,0:T(8,128)(2,1)}, u32[]{:S(2)}) copy-start(bf16[1,64,4096]{2,1,0:T(8,128)(2,1)} %references.1) | copy-start | bytes 1572868
  5.0 0.7 %copy-start.3 = (f32[8,512]{1,0:T(8,128)S(1)}, f32[8,512]{1,0:T(8,128)}, u32[]{:S(2)}) copy-start(f32[8,512]{1,0:T(8,128)} %constant.6.clone.tables) | copy-start | bytes 49156

commit v2 on v1

--- a/solution.py
+++ b/solution.py
@@ -10,6 +10,7 @@
 SIDE = 64
 MESH = pl.DeviceIdType.MESH
 CHUNKS = 8
+WINDOW = 2
 LANES = 128
 
 
@@ -190,13 +191,15 @@
 def refine_kernel(
     sizes,
     images,
-    meta,
+    class_in,
+    rotation_in,
+    defocus_in,
     tables,
-    place,
     references,
     refined,
     misfit,
     img,
+    meta,
     metas,
     crad,
     sq,
@@ -333,14 +336,22 @@
     )
     anchor_copy.start()
     pl.loop(0, chunks)(lambda index: own_copy(index).start())
+    meta[0:1] = class_in[...].astype(jnp.float32)
+    meta[1:2] = rotation_in[...].astype(jnp.float32)
+    meta[2:3] = defocus_in[...].astype(jnp.float32)
+    meta[3:8] = jnp.zeros((5, LANES), jnp.float32)
     pl.semaphore_wait(barrier, len(everyone))
     for k in range(1, 4):
         meta_copy(k).start()
-
-    @pl.loop(0, chunks)
-    def start_images(index):
+    for index in range(WINDOW):
         x_copy(index).start()
         core_copy(index).start()
+
+    @pl.loop(0, chunks)
+    def pick_radii(index):
+        target = tables[pl.ds(8 + index, 1), :width]
+        index_rows = lax.broadcasted_iota(jnp.int32, (radii, width), 0).astype(jnp.float32)
+        pick[index] = jnp.where(index_rows == target, 1.0, 0.0).astype(jnp.bfloat16)
 
     z_first = z.astype(jnp.float32)
     y_first = y.astype(jnp.float32)
@@ -384,19 +395,7 @@
     s_y_copy.start()
 
     def tick(t, carry):
-        @pl.when(t < chunks)
-        def forward():
-            x_copy(t).wait_recv()
-            forward_copy(t).start()
-            target = place[:, columns(t)]
-            index_rows = lax.broadcasted_iota(jnp.int32, (radii, width), 0).astype(jnp.float32)
-            pick[t] = jnp.where(index_rows == target, 1.0, 0.0).astype(jnp.bfloat16)
-            for block in range(4):
-                con[block, t] = jnp.dot(
-                    crad[block], pick[t], preferred_element_type=jnp.float32
-                ).astype(jnp.bfloat16)
-
-        @pl.when(t == 0)
+        @pl.when(t == 1)
         def counts_out():
             s_y_copy.wait_recv()
             total = s_own[...] + sy_got[...].astype(jnp.float32)
@@ -405,9 +404,9 @@
                 sz_send[k - 1] = total[k * share : (k + 1) * share].astype(jnp.bfloat16)
                 s_z_copy(k).start()
 
-        @pl.when((t >= 1) & (t < chunks + 1))
+        @pl.when((t >= 3) & (t < chunks + 3))
         def sum_y():
-            index = t - 1
+            index = t - 3
             y_copy(index).wait_recv()
             total = b_own[index] + y_got[index].astype(jnp.float32)
             z_own[index] = total[:share]
@@ -415,7 +414,7 @@
                 z_send[index, k - 1] = total[k * share : (k + 1) * share].astype(jnp.bfloat16)
                 z_copy(index, k).start()
 
-        @pl.when(t == 2)
+        @pl.when(t == 5)
         def counts_in():
             anchor_copy.wait()
             total = sz_own[...]
@@ -424,9 +423,9 @@
                 total = total + sz_got[k - 1].astype(jnp.float32)
             s_sum[...] = total
 
-        @pl.when((t >= 2) & (t < chunks + 2))
+        @pl.when((t >= 5) & (t < chunks + 5))
         def update():
-            index = t - 2
+            index = t - 5
             total = z_own[index]
             for k in range(1, side_z):
                 z_copy(index, k).wait_recv()
@@ -448,28 +447,23 @@
                 jnp.bfloat16
             )
 
-        @pl.when((t >= 3) & (t < chunks + 3))
+        @pl.when((t >= 7) & (t < chunks + 7))
         def spread():
-            index = t - 3
+            index = t - 7
             for k in range(1, side_z):
                 table_z_copy(index, k).wait_recv()
             table_y_copy(index).start()
 
         @pl.when(t < chunks)
-        def partial_sums():
-            own_copy(t).wait()
-            core_copy(t).wait_recv()
-            forward_copy(t).wait_recv()
+        def contrasts():
             for block in range(4):
-                work[block * LANES : (block + 1) * LANES] = con[block, t] * img[block, t]
-            total = jnp.dot(hot[...], work[...], preferred_element_type=jnp.float32)
-            b_own[t] = total[:half]
-            b_send[t] = total[half:].astype(jnp.bfloat16)
-            y_copy(t).start()
-
-        @pl.when(t >= 4)
+                con[block, t] = jnp.dot(
+                    crad[block], pick[t], preferred_element_type=jnp.float32
+                ).astype(jnp.bfloat16)
+
+        @pl.when(t >= 9)
         def residuals():
-            index = t - 4
+            index = t - 9
             table_y_copy(index).wait_recv()
             for block in range(4):
                 tiles = jnp.dot(hot_t[block], table[index], preferred_element_type=jnp.float32)
@@ -482,9 +476,32 @@
                     total = total + rest[:, part * LANES : (part + 1) * LANES]
                 acc[block] = total
 
+        @pl.when(t < chunks)
+        def forward():
+            x_copy(t).wait_recv()
+            forward_copy(t).start()
+
+        @pl.when(t < chunks - WINDOW)
+        def start_images():
+            x_copy(t + WINDOW).start()
+            core_copy(t + WINDOW).start()
+
+        @pl.when((t >= 1) & (t < chunks + 1))
+        def partial_sums():
+            index = t - 1
+            own_copy(index).wait()
+            core_copy(index).wait_recv()
+            forward_copy(index).wait_recv()
+            for block in range(4):
+                work[block * LANES : (block + 1) * LANES] = con[block, index] * img[block, index]
+            total = jnp.dot(hot[...], work[...], preferred_element_type=jnp.float32)
+            b_own[index] = total[:half]
+            b_send[index] = total[half:].astype(jnp.bfloat16)
+            y_copy(index).start()
+
         return carry
 
-    lax.fori_loop(0, chunks + 4, tick, 0)
+    lax.fori_loop(0, chunks + 9, tick, 0)
 
     for block in (1, 2, 3, 0):
         row = jnp.sum(jnp.transpose(acc[block]), axis=0, keepdims=True)
@@ -512,7 +529,7 @@
         meta_copy(k).wait_send()
         misfit_copy(k).wait()
         total = total + mis_got[k - 1]
-    misfit[...] = total
+    misfit[...] = total[0:1]
 
 
 def shards_close(side_y, side_z, images, defocus, classes, rotations, references):
@@ -525,29 +542,24 @@
     cells = side_y * half
     tables, place = radius_tables(SIDE)
     radii = tables.shape[1]
-    meta = jnp.concatenate(
-        [
-            classes.reshape(1, rows).astype(jnp.float32),
-            rotations.reshape(1, rows).astype(jnp.float32),
-            defocus.reshape(1, rows).astype(jnp.float32),
-            jnp.zeros((5, rows), jnp.float32),
-        ],
-        axis=0,
-    )
+    constants = np.zeros((8 + chunks, max(radii, width)), np.float32)
+    constants[:8, :radii] = tables
+    constants[8:, :width] = place.reshape(chunks, width)
     bf16, f32 = jnp.bfloat16, jnp.float32
     kinds = 3 + 2 * side_z
     vmem = pl.BlockSpec(memory_space=pltpu.VMEM)
-    anywhere = pl.BlockSpec(memory_space=pl.ANY)
+    anywhere = pl.BlockSpec(memory_space=pltpu.HBM)
     refined, misfit = pl.pallas_call(
         functools.partial(refine_kernel, (chunks, width, share, side_y, side_z)),
         out_shape=(
             jax.ShapeDtypeStruct((share, pixels), bf16),
-            jax.ShapeDtypeStruct((8, rows), f32),
+            jax.ShapeDtypeStruct((1, rows), f32),
         ),
-        in_specs=[anywhere, vmem, vmem, vmem, anywhere],
+        in_specs=[anywhere, vmem, vmem, vmem, vmem, anywhere],
         out_specs=(vmem, vmem),
         scratch_shapes=[
             pltpu.VMEM((4, chunks, rows, width), bf16),
+            pltpu.VMEM((8, rows), f32),
             pltpu.VMEM((3, 8, rows), f32),
             pltpu.VMEM((4, rows, radii), bf16),
             pltpu.VMEM((4 * rows, radii), bf16),
@@ -581,10 +593,17 @@
             pltpu.SemaphoreType.DMA((chunks + 1,)),
         ],
         compiler_params=pltpu.CompilerParams(
-            collective_id=0, has_side_effects=True, vmem_limit_bytes=48 * 1024 * 1024
+            collective_id=0, has_side_effects=True, vmem_limit_bytes=63 * 1024 * 1024
         ),
-    )(images, meta, jnp.asarray(tables), jnp.asarray(place), references)
-    return refined.reshape(1, share, pixels), misfit[0]
+    )(
+        images,
+        classes.reshape(1, rows),
+        rotations.reshape(1, rows),
+        defocus.reshape(1, rows),
+        jnp.asarray(constants),
+        references,
+    )
+    return refined.reshape(1, share, pixels), misfit.reshape(rows)
 
 
 def solution(mesh):

time: 71.4 us -> 58.3 us (0.82)
  Pallas kernels: 64.2 us -> 55.3 us
  local copies, waits for them, and re-layouts: 4.24 us -> 2.08 us
  other arithmetic: 2.05 us -> 0 us
    pallas_call x1, Pallas kernels: 64.2 us -> 55.3 us  [shards_close(): pl.pallas_call(functools.partial(refine_kernel, (chunks, width, share, si...]
    convert_element_type x3 -> x0, other arithmetic: 1.98 us -> none  [the longest x1 0.66 us: shards_close(): defocus.reshape(1, rows).astype(jnp.float32)]
    unnamed x9 -> x4, local copies, waits for them, and re-layouts: 3.64 us -> 2.08 us
where the time goes in v2:
time: 58.3 us; the launch traced here: 58.1 us
  Pallas kernels  55.3 us (95%)
  local copies, waits for them, and re-layouts  2.08 us (4%)
  between operations  0.65 us (1%)
    pallas_call x1, Pallas kernels, shards_close(): pl.pallas_call(functools.partial(refine_kernel, (chunks, width, share, si...  55.3 us
    unnamed x4, local copies, waits for them, and re-layouts  2.08 us

profile of v2, /device:TPU:0, one launch (start us, length us, event | category | flops | bytes accessed | tf_op | source)
XLA Modules:
  0.0 58.1 jit_solution(6523642165407394031)
XLA Ops:
  0.6 55.3 %shard_map.77 = (bf16[16,4096]{1,0:T(8,128)(2,1)}, f32[1,128]{1,0:T(1,128)}) custom-call(bf16[128,4096]{1,0:T(8,128)(2,1)} %images.1, s32[1,128]{1,0:T(1,128)} %bitcast.6, s32[1,128]{1,0:T(1,128)} %bitcast.7, bf16[1,128]{1,0:T(2,128)(2,1)} %bitcast.8, f32[16,512]{1,0:T(8,128)} %constant.2.clone.tables, bf16[1,64,4096]{2,1,0:T(8,128)(2,1)} %references.1), custom_call_target="tpu_custom_call" | custom-call | tf_op jit(solution)/shard_map/pallas_call | solution.py:552
  56.0 0.0 copy-start
  56.0 1.6 %copy.10 = bf16[1,16,4096]{2,1,0:T(8,128)(2,1)} copy(bf16[1,16,4096]{2,1,0:T(8,128)(2,1)} %bitcast.5) | data formatting | bytes 262144
  57.6 0.0 copy-done
  57.6 0.5 copy.11
Async XLA Ops:
  56.0 1.6 %copy-start = (f32[1,128]{1,0:T(1,128)S(1)}, f32[1,128]{1,0:T(1,128)}, u32[]{:S(2)}) copy-start(f32[1,128]{1,0:T(1,128)} %get-tuple-element.5) | copy-start | bytes 1540

commit v3 on v2

--- a/solution.py
+++ b/solution.py
@@ -10,7 +10,7 @@
 SIDE = 64
 MESH = pl.DeviceIdType.MESH
 CHUNKS = 8
-WINDOW = 2
+WINDOW = 4
 LANES = 128
 
 
@@ -207,7 +207,6 @@
     pick,
     hot,
     hot_t,
-    work,
     b_own,
     b_send,
     y_got,
@@ -241,14 +240,25 @@
     half = side_z * share
     cells = side_y * half
 
-    core_mate = (cls, dp + 1 - 2 * (dp % 2))
-    x_mate = (cls, (dp + 2) % 4)
-    far_mate = (cls, (dp + 2) % 4 + 1 - 2 * (dp % 2))
-    y_mate = (z * side_y + 1 - y, dp)
+    core = dp % 2
+    x = dp // 2
+    other_core = dp + 1 - 2 * core
+    other_x = dp + 2 - 4 * x
+    other_y = cls + 1 - 2 * y
+    core_mate = (cls, other_core)
+    x_mate = (cls, other_x)
+    y_mate = (other_y, dp)
+    mates = (
+        core_mate,
+        x_mate,
+        (cls, other_x + 1 - 2 * core),
+        y_mate,
+        (other_y, other_core),
+    )
     z_mates = [(((z + k) % side_z) * side_y + y, dp) for k in range(1, side_z)]
 
     barrier = pltpu.get_barrier_semaphore()
-    everyone = [core_mate, x_mate, far_mate, y_mate] + z_mates
+    everyone = list(mates) + z_mates
     for other in everyone:
         pl.semaphore_signal(barrier, inc=1, device_id=other, device_id_type=MESH)
 
@@ -272,25 +282,46 @@
             device_id_type=MESH,
         )
 
+    def share_mate(index):
+        family = index % 2
+        return (cls + family * (1 - 2 * y), dp + (1 - family) * (2 - 4 * x))
+
+    def sum_mate(index):
+        family = index % 2
+        return (cls + (1 - family) * (1 - 2 * y), dp + family * (2 - 4 * x))
+
+    def block_rows(block):
+        return pl.ds(block * LANES, LANES)
+
     def columns(index):
         return pl.ds(pl.multiple_of(index * width, width), width)
 
     def own_copy(index):
         return pltpu.make_async_copy(
-            images.at[:, columns(index)], img.at[0, index], local.at[index]
+            images.at[:, columns(index)], img.at[index, block_rows(0)], local.at[index]
         )
 
     def core_copy(index):
-        return remote(images.at[:, columns(index)], img.at[1, index], 0, index, core_mate)
-
-    def x_copy(index):
-        return remote(images.at[:, columns(index)], img.at[2, index], 1, index, x_mate)
+        return remote(
+            images.at[:, columns(index)], img.at[index, block_rows(1)], 0, index, core_mate
+        )
+
+    def share_copy(index):
+        return remote(
+            images.at[:, columns(index)],
+            img.at[index, block_rows(2)],
+            1,
+            index,
+            share_mate(index),
+        )
 
     def forward_copy(index):
-        return remote(img.at[2, index], img.at[3, index], 2, index, core_mate)
+        return remote(
+            img.at[index, block_rows(2)], img.at[index, block_rows(3)], 2, index, core_mate
+        )
 
     def y_copy(index):
-        return remote(b_send.at[index], y_got.at[index], 3, index, y_mate)
+        return remote(b_send.at[index], y_got.at[index], 3, index, sum_mate(index))
 
     def z_copy(index, k):
         return remote(
@@ -313,21 +344,19 @@
             table.at[index, pl.ds(half, half)],
             2 + 2 * side_z,
             index,
-            y_mate,
+            sum_mate(index),
         )
 
     def meta_copy(k):
-        device = (core_mate, x_mate, far_mate)[k - 1]
-        return small(meta, metas.at[k - 1], k - 1, device)
+        return small(meta, metas.at[k], k, mates[k])
 
     def misfit_copy(k):
-        device = (core_mate, x_mate, far_mate)[k - 1]
-        return small(mis.at[k], mis_got.at[k - 1], 2 + k, device)
-
-    s_y_copy = small(s_send, sy_got, 6, y_mate)
+        return small(mis.at[k], mis_got.at[k], 5 + k, mates[k])
+
+    s_y_copy = small(s_send, sy_got, 10, y_mate)
 
     def s_z_copy(k):
-        return small(sz_send.at[k - 1], sz_got.at[k - 1], 6 + k, z_mates[k - 1])
+        return small(sz_send.at[k - 1], sz_got.at[k - 1], 10 + k, z_mates[k - 1])
 
     anchor_copy = pltpu.make_async_copy(
         references.at[0, pl.ds(pl.multiple_of(dp * share, share), share)],
@@ -341,10 +370,10 @@
     meta[2:3] = defocus_in[...].astype(jnp.float32)
     meta[3:8] = jnp.zeros((5, LANES), jnp.float32)
     pl.semaphore_wait(barrier, len(everyone))
-    for k in range(1, 4):
+    for k in range(5):
         meta_copy(k).start()
     for index in range(WINDOW):
-        x_copy(index).start()
+        share_copy(index).start()
         core_copy(index).start()
 
     @pl.loop(0, chunks)
@@ -355,41 +384,48 @@
 
     z_first = z.astype(jnp.float32)
     y_first = y.astype(jnp.float32)
-    r_first = (dp * share).astype(jnp.float32)
+    x_first = x.astype(jnp.float32)
+    core_first = core.astype(jnp.float32)
     cell_rows = lax.broadcasted_iota(jnp.int32, (cells, LANES), 0).astype(jnp.float32)
     cell_lanes = lax.broadcasted_iota(jnp.int32, (LANES, cells), 1).astype(jnp.float32)
-    owned = []
-    for block in range(4):
-        if block > 0:
-            meta_copy(block).wait_recv()
-            rows = metas[block - 1]
+    owned = {}
+    for source, places in enumerate((((0, 0), (1, 0)), ((0, 1), (1, 1)), ((0, 2),), ((0, 3),), ((1, 2),), ((1, 3),))):
+        if source > 0:
+            meta_copy(source - 1).wait_recv()
+            rows = metas[source - 1]
         else:
             rows = meta[...]
-        class_row = rows[0:1]
-        rel_r = rows[1:2] - r_first
-        class_z = jnp.floor(class_row / float(side_y))
-        rel_y = jnp.abs(class_row - float(side_y) * class_z - y_first)
+        class_z = jnp.floor(rows[0:1] / float(side_y))
+        class_y = rows[0:1] - float(side_y) * class_z
+        turn_dp = jnp.floor(rows[1:2] / float(share))
+        turn_r = rows[1:2] - float(share) * turn_dp
+        turn_x = jnp.floor(turn_dp * 0.5)
         rel_z = class_z - z_first
         rel_z = jnp.where(rel_z < 0.0, rel_z + float(side_z), rel_z)
-        mine = (rel_r >= 0.0) & (rel_r < float(share))
-        cell = jnp.where(mine, rel_y * float(half) + rel_z * float(share) + rel_r, -1.0)
-        owned.append(mine)
-        hot[:, block * LANES : (block + 1) * LANES] = jnp.where(cell_rows == cell, 1.0, 0.0).astype(
-            jnp.bfloat16
-        )
-        cell_t = jnp.transpose(jnp.broadcast_to(cell, (LANES, LANES)))
-        hot_t[block] = jnp.where(cell_lanes == cell_t, 1.0, 0.0).astype(jnp.bfloat16)
+        off_x = jnp.abs(turn_x - x_first)
+        off_y = jnp.abs(class_y - y_first)
+        off_core = jnp.abs(turn_dp - 2.0 * turn_x - core_first)
         focus = jnp.transpose(jnp.broadcast_to(rows[2:3], (LANES, LANES)))
+        for family, block in places:
+            off_share, off_sum = (off_x, off_y) if family == 0 else (off_y, off_x)
+            mine = (off_share + off_core) < 0.5
+            cell = jnp.where(mine, off_sum * float(half) + rel_z * float(share) + turn_r, -1.0)
+            owned[family, block] = mine
+            span = slice(block * LANES, (block + 1) * LANES)
+            hot[family, :, span] = jnp.where(cell_rows == cell, 1.0, 0.0).astype(jnp.bfloat16)
+            cell_t = jnp.transpose(jnp.broadcast_to(cell, (LANES, LANES)))
+            hot_t[family, span] = jnp.where(cell_lanes == cell_t, 1.0, 0.0).astype(jnp.bfloat16)
         for part in range(radii // LANES):
             lanes = slice(part * LANES, (part + 1) * LANES)
             phase = 20.0 * focus * tables[0:1, lanes] + 0.1
             wave = bounded_sine(phase) * tables[1:2, lanes]
-            crad[block, :, lanes] = wave.astype(jnp.bfloat16)
-            sq[block * LANES : (block + 1) * LANES, lanes] = (
-                wave * wave + tables[2:3, lanes]
-            ).astype(jnp.bfloat16)
+            for family, block in places:
+                span = slice(block * LANES, (block + 1) * LANES)
+                crad[family, span, lanes] = wave.astype(jnp.bfloat16)
+                if family == 0:
+                    sq[span, lanes] = (wave * wave + tables[2:3, lanes]).astype(jnp.bfloat16)
     acc[...] = jnp.zeros_like(acc)
-    partial = jnp.dot(hot[...], sq[...], preferred_element_type=jnp.float32)
+    partial = jnp.dot(hot[0], sq[...], preferred_element_type=jnp.float32)
     s_own[...] = partial[:half]
     s_send[...] = partial[half:].astype(jnp.bfloat16)
     s_y_copy.start()
@@ -433,8 +469,12 @@
             squares = s_sum[...]
             coarse = squares.astype(jnp.bfloat16)
             fine = (squares - coarse.astype(jnp.float32)).astype(jnp.bfloat16)
-            energy = jnp.dot(coarse, pick[index], preferred_element_type=jnp.float32)
-            energy = energy + jnp.dot(fine, pick[index], preferred_element_type=jnp.float32)
+            pair = jnp.dot(
+                jnp.concatenate([coarse, fine], axis=0),
+                pick[index],
+                preferred_element_type=jnp.float32,
+            )
+            energy = pair[:share] + pair[share:]
             damping = 0.5 * squares[:, radii - 1 : radii] + 1.0
             scale = 1.0 / damping
             start = anchor[:, columns(index)].astype(jnp.float32)
@@ -456,34 +496,30 @@
 
         @pl.when(t < chunks)
         def contrasts():
-            for block in range(4):
-                con[block, t] = jnp.dot(
-                    crad[block], pick[t], preferred_element_type=jnp.float32
-                ).astype(jnp.bfloat16)
+            con[t] = jnp.dot(
+                crad[t % 2], pick[t], preferred_element_type=jnp.float32
+            ).astype(jnp.bfloat16)
 
         @pl.when(t >= 9)
         def residuals():
             index = t - 9
             table_y_copy(index).wait_recv()
-            for block in range(4):
-                tiles = jnp.dot(hot_t[block], table[index], preferred_element_type=jnp.float32)
-                rest = con[block, index].astype(jnp.float32) * tiles - img[block, index].astype(
-                    jnp.float32
-                )
-                rest = rest * rest
-                total = acc[block]
-                for part in range(width // LANES):
-                    total = total + rest[:, part * LANES : (part + 1) * LANES]
-                acc[block] = total
+            tiles = jnp.dot(hot_t[index % 2], table[index], preferred_element_type=jnp.float32)
+            rest = con[index].astype(jnp.float32) * tiles - img[index].astype(jnp.float32)
+            rest = rest * rest
+            total = acc[index % 2]
+            for part in range(width // LANES):
+                total = total + rest[:, part * LANES : (part + 1) * LANES]
+            acc[index % 2] = total
 
         @pl.when(t < chunks)
         def forward():
-            x_copy(t).wait_recv()
+            share_copy(t).wait_recv()
             forward_copy(t).start()
 
         @pl.when(t < chunks - WINDOW)
         def start_images():
-            x_copy(t + WINDOW).start()
+            share_copy(t + WINDOW).start()
             core_copy(t + WINDOW).start()
 
         @pl.when((t >= 1) & (t < chunks + 1))
@@ -492,9 +528,9 @@
             own_copy(index).wait()
             core_copy(index).wait_recv()
             forward_copy(index).wait_recv()
-            for block in range(4):
-                work[block * LANES : (block + 1) * LANES] = con[block, index] * img[block, index]
-            total = jnp.dot(hot[...], work[...], preferred_element_type=jnp.float32)
+            total = jnp.dot(
+                hot[index % 2], con[index] * img[index], preferred_element_type=jnp.float32
+            )
             b_own[index] = total[:half]
             b_send[index] = total[half:].astype(jnp.bfloat16)
             y_copy(index).start()
@@ -503,17 +539,27 @@
 
     lax.fori_loop(0, chunks + 9, tick, 0)
 
-    for block in (1, 2, 3, 0):
-        row = jnp.sum(jnp.transpose(acc[block]), axis=0, keepdims=True)
-        row = jnp.where(owned[block], row * (1.0 / float(chunks * width)), 0.0)
-        mis[block] = jnp.broadcast_to(row, mis.shape[1:])
-        if block > 0:
-            misfit_copy(block).start()
+    def row_of(family, block):
+        part = acc[family, block * LANES : (block + 1) * LANES]
+        row = jnp.sum(jnp.transpose(part), axis=0, keepdims=True)
+        return jnp.where(owned[family, block], row * (1.0 / float(chunks * width)), 0.0)
+
+    for k, row in enumerate(
+        (
+            row_of(0, 1) + row_of(1, 1),
+            row_of(0, 2),
+            row_of(0, 3),
+            row_of(1, 2),
+            row_of(1, 3),
+        )
+    ):
+        mis[k] = jnp.broadcast_to(row, mis.shape[1:])
+        misfit_copy(k).start()
 
     @pl.loop(0, chunks)
     def drain(index):
         core_copy(index).wait_send()
-        x_copy(index).wait_send()
+        share_copy(index).wait_send()
         forward_copy(index).wait_send()
         y_copy(index).wait_send()
         for k in range(1, side_z):
@@ -524,12 +570,12 @@
     s_y_copy.wait_send()
     for k in range(1, side_z):
         s_z_copy(k).wait_send()
-    total = mis[0]
-    for k in range(1, 4):
+    total = row_of(0, 0) + row_of(1, 0)
+    for k in range(5):
         meta_copy(k).wait_send()
         misfit_copy(k).wait()
-        total = total + mis_got[k - 1]
-    misfit[...] = total[0:1]
+        total = total + mis_got[k, 0:1]
+    misfit[...] = total
 
 
 def shards_close(side_y, side_z, images, defocus, classes, rotations, references):
@@ -558,16 +604,15 @@
         in_specs=[anywhere, vmem, vmem, vmem, vmem, anywhere],
         out_specs=(vmem, vmem),
         scratch_shapes=[
-            pltpu.VMEM((4, chunks, rows, width), bf16),
+            pltpu.VMEM((chunks, 4 * rows, width), bf16),
             pltpu.VMEM((8, rows), f32),
-            pltpu.VMEM((3, 8, rows), f32),
-            pltpu.VMEM((4, rows, radii), bf16),
+            pltpu.VMEM((5, 8, rows), f32),
+            pltpu.VMEM((2, 4 * rows, radii), bf16),
             pltpu.VMEM((4 * rows, radii), bf16),
-            pltpu.VMEM((4, chunks, rows, width), bf16),
+            pltpu.VMEM((chunks, 4 * rows, width), bf16),
             pltpu.VMEM((chunks, radii, width), bf16),
-            pltpu.VMEM((cells, 4 * rows), bf16),
-            pltpu.VMEM((4, rows, cells), bf16),
-            pltpu.VMEM((4 * rows, width), bf16),
+            pltpu.VMEM((2, cells, 4 * rows), bf16),
+            pltpu.VMEM((2, 4 * rows, cells), bf16),
             pltpu.VMEM((chunks, half, width), f32),
             pltpu.VMEM((chunks, half, width), bf16),
             pltpu.VMEM((chunks, half, width), bf16),
@@ -583,13 +628,13 @@
             pltpu.VMEM((side_z - 1, share, radii), bf16),
             pltpu.VMEM((share, radii), f32),
             pltpu.VMEM((share, pixels), bf16),
-            pltpu.VMEM((4, rows, LANES), f32),
-            pltpu.VMEM((4, 8, rows), f32),
-            pltpu.VMEM((3, 8, rows), f32),
+            pltpu.VMEM((2, 4 * rows, LANES), f32),
+            pltpu.VMEM((5, 8, rows), f32),
+            pltpu.VMEM((5, 8, rows), f32),
             pltpu.SemaphoreType.DMA((kinds, chunks)),
             pltpu.SemaphoreType.DMA((kinds, chunks)),
-            pltpu.SemaphoreType.DMA((6 + side_z,)),
-            pltpu.SemaphoreType.DMA((6 + side_z,)),
+            pltpu.SemaphoreType.DMA((10 + side_z,)),
+            pltpu.SemaphoreType.DMA((10 + side_z,)),
             pltpu.SemaphoreType.DMA((chunks + 1,)),
         ],
         compiler_params=pltpu.CompilerParams(

time: 58.3 us -> 60.8 us (1.043)
  Pallas kernels: 55.3 us -> 57.8 us
    pallas_call x1, Pallas kernels: 55.3 us -> 57.8 us  [shards_close(): pl.pallas_call(functools.partial(refine_kernel, (chunks, width, share, si...]
where the time goes in v3:
time: 60.8 us; the launch traced here: 60.6 us
  Pallas kernels  57.8 us (95%)
  local copies, waits for them, and re-layouts  2.08 us (3%)
  between operations  0.65 us (1%)
    pallas_call x1, Pallas kernels, shards_close(): pl.pallas_call(functools.partial(refine_kernel, (chunks, width, share, si...  57.8 us
    unnamed x4, local copies, waits for them, and re-layouts  2.08 us

profile of v3, /device:TPU:0, one launch (start us, length us, event | category | flops | bytes accessed | tf_op | source)
XLA Modules:
  0.0 60.6 jit_solution(14391610716180048819)
XLA Ops:
  0.6 57.8 %shard_map.77 = (bf16[16,4096]{1,0:T(8,128)(2,1)}, f32[1,128]{1,0:T(1,128)}) custom-call(bf16[128,4096]{1,0:T(8,128)(2,1)} %images.1, s32[1,128]{1,0:T(1,128)} %bitcast.6, s32[1,128]{1,0:T(1,128)} %bitcast.7, bf16[1,128]{1,0:T(2,128)(2,1)} %bitcast.8, f32[16,512]{1,0:T(8,128)} %constant.2.clone.tables, bf16[1,64,4096]{2,1,0:T(8,128)(2,1)} %references.1), custom_call_target="tpu_custom_call" | custom-call | tf_op jit(solution)/shard_map/pallas_call | solution.py:598
  58.5 0.0 copy-start
  58.5 1.6 %copy.10 = bf16[1,16,4096]{2,1,0:T(8,128)(2,1)} copy(bf16[1,16,4096]{2,1,0:T(8,128)(2,1)} %bitcast.5) | data formatting | bytes 262144
  60.0 0.0 copy-done
  60.0 0.5 copy.11
Async XLA Ops:
  58.5 1.6 %copy-start = (f32[1,128]{1,0:T(1,128)S(1)}, f32[1,128]{1,0:T(1,128)}, u32[]{:S(2)}) copy-start(f32[1,128]{1,0:T(1,128)} %get-tuple-element.5) | copy-start | bytes 1540

commit v4 on v3

--- a/solution.py
+++ b/solution.py
@@ -9,7 +9,7 @@
 
 SIDE = 64
 MESH = pl.DeviceIdType.MESH
-CHUNKS = 8
+CHUNKS = 4
 WINDOW = 4
 LANES = 128
 

time: 60.8 us -> 61.3 us (level)
  no operation moved by 1% of the time
where the time goes in v4:
time: 61.3 us; the launch traced here: 61.1 us
  Pallas kernels  58.4 us (95%)
  local copies, waits for them, and re-layouts  2.08 us (3%)
  between operations  0.65 us (1%)
    pallas_call x1, Pallas kernels, shards_close(): pl.pallas_call(functools.partial(refine_kernel, (chunks, width, share, si...  58.4 us
    unnamed x4, local copies, waits for them, and re-layouts  2.08 us

profile of v4, /device:TPU:0, one launch (start us, length us, event | category | flops | bytes accessed | tf_op | source)
XLA Modules:
  0.0 61.1 jit_solution(15397914798301196355)
XLA Ops:
  0.6 58.4 %shard_map.77 = (bf16[16,4096]{1,0:T(8,128)(2,1)}, f32[1,128]{1,0:T(1,128)}) custom-call(bf16[128,4096]{1,0:T(8,128)(2,1)} %images.1, s32[1,128]{1,0:T(1,128)} %bitcast.6, s32[1,128]{1,0:T(1,128)} %bitcast.7, bf16[1,128]{1,0:T(2,128)(2,1)} %bitcast.8, f32[12,1024]{1,0:T(8,128)} %constant.2.clone.tables, bf16[1,64,4096]{2,1,0:T(8,128)(2,1)} %references.1), custom_call_target="tpu_custom_call" | custom-call | tf_op jit(solution)/shard_map/pallas_call | solution.py:598
  59.0 0.0 copy-start
  59.0 1.6 %copy.10 = bf16[1,16,4096]{2,1,0:T(8,128)(2,1)} copy(bf16[1,16,4096]{2,1,0:T(8,128)(2,1)} %bitcast.5) | data formatting | bytes 262144
  60.6 0.0 copy-done
  60.6 0.5 copy.11
Async XLA Ops:
  59.0 1.6 %copy-start = (f32[1,128]{1,0:T(1,128)S(1)}, f32[1,128]{1,0:T(1,128)}, u32[]{:S(2)}) copy-start(f32[1,128]{1,0:T(1,128)} %get-tuple-element.5) | copy-start | bytes 1540

commit v5 on v3

--- a/solution.py
+++ b/solution.py
@@ -364,7 +364,11 @@
         local.at[chunks],
     )
     anchor_copy.start()
-    pl.loop(0, chunks)(lambda index: own_copy(index).start())
+
+    @pl.loop(0, chunks)
+    def start_local(index):
+        own_copy(index).start()
+
     meta[0:1] = class_in[...].astype(jnp.float32)
     meta[1:2] = rotation_in[...].astype(jnp.float32)
     meta[2:3] = defocus_in[...].astype(jnp.float32)
@@ -376,11 +380,19 @@
         share_copy(index).start()
         core_copy(index).start()
 
+    index_rows = lax.broadcasted_iota(jnp.int32, (LANES, LANES), 0).astype(jnp.float32)
+
     @pl.loop(0, chunks)
     def pick_radii(index):
-        target = tables[pl.ds(8 + index, 1), :width]
-        index_rows = lax.broadcasted_iota(jnp.int32, (radii, width), 0).astype(jnp.float32)
-        pick[index] = jnp.where(index_rows == target, 1.0, 0.0).astype(jnp.bfloat16)
+        row = tables[pl.ds(8 + index, 1), :width]
+        for part in range(width // LANES):
+            lanes = slice(part * LANES, (part + 1) * LANES)
+            target = jnp.broadcast_to(row[:, lanes], (LANES, LANES))
+            for block in range(radii // LANES):
+                match = index_rows == target - float(block * LANES)
+                pick[index, block * LANES : (block + 1) * LANES, lanes] = jnp.where(
+                    match, 1.0, 0.0
+                ).astype(jnp.bfloat16)
 
     z_first = z.astype(jnp.float32)
     y_first = y.astype(jnp.float32)
@@ -483,9 +495,7 @@
             for k in range(1, side_z):
                 table_z_copy(index, k).start()
             again = first.astype(jnp.float32)
-            refined[:, columns(index)] = (again - (again * energy - total) * scale).astype(
-                jnp.bfloat16
-            )
+            refined[:, columns(index)] = again - (again * energy - total) * scale
 
         @pl.when((t >= 7) & (t < chunks + 7))
         def spread():
@@ -496,21 +506,28 @@
 
         @pl.when(t < chunks)
         def contrasts():
-            con[t] = jnp.dot(
-                crad[t % 2], pick[t], preferred_element_type=jnp.float32
-            ).astype(jnp.bfloat16)
+            for block in range(2):
+                span = pl.ds(2 * block * LANES, 2 * LANES)
+                con[t, span] = jnp.dot(
+                    crad[t % 2, span], pick[t], preferred_element_type=jnp.float32
+                ).astype(jnp.bfloat16)
 
         @pl.when(t >= 9)
         def residuals():
             index = t - 9
             table_y_copy(index).wait_recv()
-            tiles = jnp.dot(hot_t[index % 2], table[index], preferred_element_type=jnp.float32)
-            rest = con[index].astype(jnp.float32) * tiles - img[index].astype(jnp.float32)
-            rest = rest * rest
-            total = acc[index % 2]
-            for part in range(width // LANES):
-                total = total + rest[:, part * LANES : (part + 1) * LANES]
-            acc[index % 2] = total
+            for block in range(4):
+                span = block_rows(block)
+                tiles = jnp.dot(
+                    hot_t[index % 2, span], table[index], preferred_element_type=jnp.float32
+                )
+                total = acc[index % 2, span]
+                for part in range(width // LANES):
+                    lanes = slice(part * LANES, (part + 1) * LANES)
+                    rest = con[index, span, lanes].astype(jnp.float32) * tiles[:, lanes]
+                    rest = rest - img[index, span, lanes].astype(jnp.float32)
+                    total = total + rest * rest
+                acc[index % 2, span] = total
 
         @pl.when(t < chunks)
         def forward():
@@ -598,7 +615,7 @@
     refined, misfit = pl.pallas_call(
         functools.partial(refine_kernel, (chunks, width, share, side_y, side_z)),
         out_shape=(
-            jax.ShapeDtypeStruct((share, pixels), bf16),
+            jax.ShapeDtypeStruct((share, pixels), f32),
             jax.ShapeDtypeStruct((1, rows), f32),
         ),
         in_specs=[anywhere, vmem, vmem, vmem, vmem, anywhere],
@@ -648,7 +665,7 @@
         jnp.asarray(constants),
         references,
     )
-    return refined.reshape(1, share, pixels), misfit.reshape(rows)
+    return refined.astype(bf16).reshape(1, share, pixels), misfit.reshape(rows)
 
 
 def solution(mesh):

time: 60.8 us -> 61.5 us (1.012)
  other arithmetic: 0 us -> 1.62 us
  local copies, waits for them, and re-layouts: 2.08 us -> 1.08 us
    reshape x0 -> x1, other arithmetic: none -> 1.62 us  [shards_close(): refined.astype(bf16).reshape(1, share, pixels)]
    unnamed x4 -> x3, local copies, waits for them, and re-layouts: 2.08 us -> 1.08 us
where the time goes in v5:
time: 61.5 us; the launch traced here: 61.3 us
  Pallas kernels  57.9 us (94%)
  other arithmetic  1.62 us (3%)
  local copies, waits for them, and re-layouts  1.08 us (2%)
  between operations  0.64 us (1%)
    pallas_call x1, Pallas kernels, shards_close(): pl.pallas_call(functools.partial(refine_kernel, (chunks, width, share, si...  57.9 us
    reshape x1, other arithmetic, shards_close(): refined.astype(bf16).reshape(1, share, pixels)  1.62 us

profile of v5, /device:TPU:0, one launch (start us, length us, event | category | flops | bytes accessed | tf_op | source)
XLA Modules:
  0.0 61.3 jit_solution(13968825511712121951)
XLA Ops:
  0.6 57.9 %shard_map.77 = (f32[16,4096]{1,0:T(8,128)}, f32[1,128]{1,0:T(1,128)}) custom-call(bf16[128,4096]{1,0:T(8,128)(2,1)} %images.1, s32[1,128]{1,0:T(1,128)} %bitcast.6, s32[1,128]{1,0:T(1,128)} %bitcast.7, bf16[1,128]{1,0:T(2,128)(2,1)} %bitcast.8, f32[16,512]{1,0:T(8,128)} %constant.2.clone.tables, bf16[1,64,4096]{2,1,0:T(8,128)(2,1)} %references.1), custom_call_target="tpu_custom_call" | custom-call | tf_op jit(solution)/shard_map/pallas_call | solution.py:615
  58.6 1.6 %convert_bitcast_fusion = bf16[1,16,4096]{2,1,0:T(8,128)(2,1)} fusion(f32[16,4096]{1,0:T(8,128)} %get-tuple-element.4), kind=kLoop, calls=%fused_computation | loop fusion | flops 65536 | bytes 393216 | tf_op jit(solution)/shard_map/reshape | solution.py:668
  60.2 0.0 copy-start
  60.2 0.6 copy-done
  60.7 0.5 copy.9
Async XLA Ops:
  60.2 0.6 copy-start

commit v6 on v5

--- a/solution.py
+++ b/solution.py
@@ -11,6 +11,15 @@
 MESH = pl.DeviceIdType.MESH
 CHUNKS = 8
 WINDOW = 4
+FAMILIES = 1
+SINE = (
+    6.283182792843448,
+    -41.341419333015786,
+    81.59613740878902,
+    -76.57967400034848,
+    41.203682075135006,
+    -12.268761447374176,
+)
 LANES = 128
 
 
@@ -168,24 +177,18 @@
     rows = np.zeros((8, width), np.float32)
     rows[0, : len(values)] = values.astype(np.float32) / np.float32(half_side * half_side)
     rows[1, : len(values)] = -np.exp(-0.5 * rows[0, : len(values)])
+    rows[0] = (rows[0].astype(np.float64) * (10.0 / np.pi)).astype(np.float32)
     rows[2, width - 1] = 1.0
     return rows, place.reshape(1, -1).astype(np.float32)
 
 
-def bounded_sine(angle):
-    turns = jnp.floor(angle * np.float32(1.0 / np.pi) + 0.5)
-    rest = angle - turns * np.float32(3.140625)
-    rest = rest - turns * np.float32(9.67502593994140625e-4)
-    rest = rest - turns * np.float32(1.509957990978376432e-7)
-    odd = turns - 2.0 * jnp.floor(turns * 0.5)
-    sign = 1.0 - 2.0 * odd
+def sine_of_turns(turns):
+    rest = turns - jnp.floor(turns + 0.5)
     square = rest * rest
-    poly = np.float32(-2.3889859e-08)
-    poly = poly * square + np.float32(2.7525562e-06)
-    poly = poly * square + np.float32(-1.9840874e-04)
-    poly = poly * square + np.float32(8.3333310e-03)
-    poly = poly * square + np.float32(-1.6666667e-01)
-    return sign * (rest + rest * square * poly)
+    poly = np.float32(SINE[-1])
+    for term in SINE[-2::-1]:
+        poly = poly * square + np.float32(term)
+    return rest * poly
 
 
 def refine_kernel(
@@ -258,7 +261,10 @@
     z_mates = [(((z + k) % side_z) * side_y + y, dp) for k in range(1, side_z)]
 
     barrier = pltpu.get_barrier_semaphore()
-    everyone = list(mates) + z_mates
+    friends = 1 + 2 * FAMILIES
+    everyone = list(mates[:friends]) + z_mates
+    if FAMILIES == 1:
+        everyone.append(y_mate)
     for other in everyone:
         pl.semaphore_signal(barrier, inc=1, device_id=other, device_id_type=MESH)
 
@@ -283,11 +289,11 @@
         )
 
     def share_mate(index):
-        family = index % 2
+        family = index % FAMILIES
         return (cls + family * (1 - 2 * y), dp + (1 - family) * (2 - 4 * x))
 
     def sum_mate(index):
-        family = index % 2
+        family = index % FAMILIES
         return (cls + (1 - family) * (1 - 2 * y), dp + family * (2 - 4 * x))
 
     def block_rows(block):
@@ -374,7 +380,7 @@
     meta[2:3] = defocus_in[...].astype(jnp.float32)
     meta[3:8] = jnp.zeros((5, LANES), jnp.float32)
     pl.semaphore_wait(barrier, len(everyone))
-    for k in range(5):
+    for k in range(friends):
         meta_copy(k).start()
     for index in range(WINDOW):
         share_copy(index).start()
@@ -401,7 +407,9 @@
     cell_rows = lax.broadcasted_iota(jnp.int32, (cells, LANES), 0).astype(jnp.float32)
     cell_lanes = lax.broadcasted_iota(jnp.int32, (LANES, cells), 1).astype(jnp.float32)
     owned = {}
-    for source, places in enumerate((((0, 0), (1, 0)), ((0, 1), (1, 1)), ((0, 2),), ((0, 3),), ((1, 2),), ((1, 3),))):
+    groups = (((0, 0), (1, 0)), ((0, 1), (1, 1)), ((0, 2),), ((0, 3),), ((1, 2),), ((1, 3),))
+    for source in range(friends + 1):
+        places = [place for place in groups[source] if place[0] < FAMILIES]
         if source > 0:
             meta_copy(source - 1).wait_recv()
             rows = metas[source - 1]
@@ -429,21 +437,17 @@
             hot_t[family, span] = jnp.where(cell_lanes == cell_t, 1.0, 0.0).astype(jnp.bfloat16)
         for part in range(radii // LANES):
             lanes = slice(part * LANES, (part + 1) * LANES)
-            phase = 20.0 * focus * tables[0:1, lanes] + 0.1
-            wave = bounded_sine(phase) * tables[1:2, lanes]
+            turns = focus * tables[0:1, lanes] + np.float32(0.1 / (2.0 * np.pi))
+            wave = sine_of_turns(turns) * tables[1:2, lanes]
             for family, block in places:
                 span = slice(block * LANES, (block + 1) * LANES)
                 crad[family, span, lanes] = wave.astype(jnp.bfloat16)
                 if family == 0:
                     sq[span, lanes] = (wave * wave + tables[2:3, lanes]).astype(jnp.bfloat16)
     acc[...] = jnp.zeros_like(acc)
-    partial = jnp.dot(hot[0], sq[...], preferred_element_type=jnp.float32)
-    s_own[...] = partial[:half]
-    s_send[...] = partial[half:].astype(jnp.bfloat16)
-    s_y_copy.start()
 
     def tick(t, carry):
-        @pl.when(t == 1)
+        @pl.when(t == 3)
         def counts_out():
             s_y_copy.wait_recv()
             total = s_own[...] + sy_got[...].astype(jnp.float32)
@@ -495,7 +499,9 @@
             for k in range(1, side_z):
                 table_z_copy(index, k).start()
             again = first.astype(jnp.float32)
-            refined[:, columns(index)] = again - (again * energy - total) * scale
+            refined[:, columns(index)] = (again - (again * energy - total) * scale).astype(
+                jnp.bfloat16
+            )
 
         @pl.when((t >= 7) & (t < chunks + 7))
         def spread():
@@ -509,7 +515,7 @@
             for block in range(2):
                 span = pl.ds(2 * block * LANES, 2 * LANES)
                 con[t, span] = jnp.dot(
-                    crad[t % 2, span], pick[t], preferred_element_type=jnp.float32
+                    crad[t % FAMILIES, span], pick[t], preferred_element_type=jnp.float32
                 ).astype(jnp.bfloat16)
 
         @pl.when(t >= 9)
@@ -519,15 +525,15 @@
             for block in range(4):
                 span = block_rows(block)
                 tiles = jnp.dot(
-                    hot_t[index % 2, span], table[index], preferred_element_type=jnp.float32
+                    hot_t[index % FAMILIES, span], table[index], preferred_element_type=jnp.float32
                 )
-                total = acc[index % 2, span]
+                total = acc[index % FAMILIES, span]
                 for part in range(width // LANES):
                     lanes = slice(part * LANES, (part + 1) * LANES)
                     rest = con[index, span, lanes].astype(jnp.float32) * tiles[:, lanes]
                     rest = rest - img[index, span, lanes].astype(jnp.float32)
                     total = total + rest * rest
-                acc[index % 2, span] = total
+                acc[index % FAMILIES, span] = total
 
         @pl.when(t < chunks)
         def forward():
@@ -546,12 +552,19 @@
             core_copy(index).wait_recv()
             forward_copy(index).wait_recv()
             total = jnp.dot(
-                hot[index % 2], con[index] * img[index], preferred_element_type=jnp.float32
+                hot[index % FAMILIES], con[index] * img[index], preferred_element_type=jnp.float32
             )
             b_own[index] = total[:half]
             b_send[index] = total[half:].astype(jnp.bfloat16)
             y_copy(index).start()
 
+        @pl.when(t == 1)
+        def counts_start():
+            partial = jnp.dot(hot[0], sq[...], preferred_element_type=jnp.float32)
+            s_own[...] = partial[:half]
+            s_send[...] = partial[half:].astype(jnp.bfloat16)
+            s_y_copy.start()
+
         return carry
 
     lax.fori_loop(0, chunks + 9, tick, 0)
@@ -561,15 +574,11 @@
         row = jnp.sum(jnp.transpose(part), axis=0, keepdims=True)
         return jnp.where(owned[family, block], row * (1.0 / float(chunks * width)), 0.0)
 
-    for k, row in enumerate(
-        (
-            row_of(0, 1) + row_of(1, 1),
-            row_of(0, 2),
-            row_of(0, 3),
-            row_of(1, 2),
-            row_of(1, 3),
-        )
-    ):
+    rows_out = [row_of(0, 1), row_of(0, 2), row_of(0, 3)]
+    if FAMILIES == 2:
+        rows_out[0] = rows_out[0] + row_of(1, 1)
+        rows_out = rows_out + [row_of(1, 2), row_of(1, 3)]
+    for k, row in enumerate(rows_out):
         mis[k] = jnp.broadcast_to(row, mis.shape[1:])
         misfit_copy(k).start()
 
@@ -587,8 +596,10 @@
     s_y_copy.wait_send()
     for k in range(1, side_z):
         s_z_copy(k).wait_send()
-    total = row_of(0, 0) + row_of(1, 0)
-    for k in range(5):
+    total = row_of(0, 0)
+    if FAMILIES == 2:
+        total = total + row_of(1, 0)
+    for k in range(friends):
         meta_copy(k).wait_send()
         misfit_copy(k).wait()
         total = total + mis_got[k, 0:1]
@@ -615,7 +626,7 @@
     refined, misfit = pl.pallas_call(
         functools.partial(refine_kernel, (chunks, width, share, side_y, side_z)),
         out_shape=(
-            jax.ShapeDtypeStruct((share, pixels), f32),
+            jax.ShapeDtypeStruct((share, pixels), bf16),
             jax.ShapeDtypeStruct((1, rows), f32),
         ),
         in_specs=[anywhere, vmem, vmem, vmem, vmem, anywhere],
@@ -623,13 +634,13 @@
         scratch_shapes=[
             pltpu.VMEM((chunks, 4 * rows, width), bf16),
             pltpu.VMEM((8, rows), f32),
-            pltpu.VMEM((5, 8, rows), f32),
-            pltpu.VMEM((2, 4 * rows, radii), bf16),
+            pltpu.VMEM((1 + 2 * FAMILIES, 8, rows), f32),
+            pltpu.VMEM((FAMILIES, 4 * rows, radii), bf16),
             pltpu.VMEM((4 * rows, radii), bf16),
             pltpu.VMEM((chunks, 4 * rows, width), bf16),
             pltpu.VMEM((chunks, radii, width), bf16),
-            pltpu.VMEM((2, cells, 4 * rows), bf16),
-            pltpu.VMEM((2, 4 * rows, cells), bf16),
+            pltpu.VMEM((FAMILIES, cells, 4 * rows), bf16),
+            pltpu.VMEM((FAMILIES, 4 * rows, cells), bf16),
             pltpu.VMEM((chunks, half, width), f32),
             pltpu.VMEM((chunks, half, width), bf16),
             pltpu.VMEM((chunks, half, width), bf16),
@@ -645,9 +656,9 @@
             pltpu.VMEM((side_z - 1, share, radii), bf16),
             pltpu.VMEM((share, radii), f32),
             pltpu.VMEM((share, pixels), bf16),
-            pltpu.VMEM((2, 4 * rows, LANES), f32),
-            pltpu.VMEM((5, 8, rows), f32),
-            pltpu.VMEM((5, 8, rows), f32),
+            pltpu.VMEM((FAMILIES, 4 * rows, LANES), f32),
+            pltpu.VMEM((1 + 2 * FAMILIES, 8, rows), f32),
+            pltpu.VMEM((1 + 2 * FAMILIES, 8, rows), f32),
             pltpu.SemaphoreType.DMA((kinds, chunks)),
             pltpu.SemaphoreType.DMA((kinds, chunks)),
             pltpu.SemaphoreType.DMA((10 + side_z,)),
@@ -665,7 +676,7 @@
         jnp.asarray(constants),
         references,
     )
-    return refined.astype(bf16).reshape(1, share, pixels), misfit.reshape(rows)
+    return refined.reshape(1, share, pixels), misfit.reshape(rows)
 
 
 def solution(mesh):

time: 61.5 us -> 58.7 us (0.954)
  Pallas kernels: 57.9 us -> 55.8 us
  other arithmetic: 1.62 us -> 0 us
  local copies, waits for them, and re-layouts: 1.08 us -> 2.08 us
    pallas_call x1, Pallas kernels: 57.9 us -> 55.8 us  [shards_close(): pl.pallas_call(functools.partial(refine_kernel, (chunks, width, share, si...]
    reshape x1 -> x0, other arithmetic: 1.62 us -> none  [shards_close(): refined.astype(bf16).reshape(1, share, pixels)]
    unnamed x3 -> x4, local copies, waits for them, and re-layouts: 1.08 us -> 2.08 us
where the time goes in v6:
time: 58.7 us; the launch traced here: 58.5 us
  Pallas kernels  55.8 us (95%)
  local copies, waits for them, and re-layouts  2.08 us (4%)
  between operations  0.65 us (1%)
    pallas_call x1, Pallas kernels, shards_close(): pl.pallas_call(functools.partial(refine_kernel, (chunks, width, share, si...  55.8 us
    unnamed x4, local copies, waits for them, and re-layouts  2.08 us

profile of v6, /device:TPU:0, one launch (start us, length us, event | category | flops | bytes accessed | tf_op | source)
XLA Modules:
  0.0 58.5 jit_solution(379084933897819853)
XLA Ops:
  0.6 55.8 %shard_map.77 = (bf16[16,4096]{1,0:T(8,128)(2,1)}, f32[1,128]{1,0:T(1,128)}) custom-call(bf16[128,4096]{1,0:T(8,128)(2,1)} %images.1, s32[1,128]{1,0:T(1,128)} %bitcast.6, s32[1,128]{1,0:T(1,128)} %bitcast.7, bf16[1,128]{1,0:T(2,128)(2,1)} %bitcast.8, f32[16,512]{1,0:T(8,128)} %constant.2.clone.tables, bf16[1,64,4096]{2,1,0:T(8,128)(2,1)} %references.1), custom_call_target="tpu_custom_call" | custom-call | tf_op jit(solution)/shard_map/pallas_call | solution.py:626
  56.4 0.0 copy-start
  56.4 1.6 %copy.10 = bf16[1,16,4096]{2,1,0:T(8,128)(2,1)} copy(bf16[1,16,4096]{2,1,0:T(8,128)(2,1)} %bitcast.5) | data formatting | bytes 262144
  58.0 0.0 copy-done
  58.0 0.5 copy.11
Async XLA Ops:
  56.4 1.6 %copy-start = (f32[1,128]{1,0:T(1,128)S(1)}, f32[1,128]{1,0:T(1,128)}, u32[]{:S(2)}) copy-start(f32[1,128]{1,0:T(1,128)} %get-tuple-element.5) | copy-start | bytes 1540

commit v7 on v6

--- a/solution.py
+++ b/solution.py
@@ -10,7 +10,7 @@
 SIDE = 64
 MESH = pl.DeviceIdType.MESH
 CHUNKS = 8
-WINDOW = 4
+WINDOW = 2
 FAMILIES = 1
 SINE = (
     6.283182792843448,

time: 58.7 us -> 58.6 us (level)
  no operation moved by 1% of the time
where the time goes in v7:
time: 58.6 us; the launch traced here: 58.4 us
  Pallas kernels  55.7 us (95%)
  local copies, waits for them, and re-layouts  2.08 us (4%)
  between operations  0.65 us (1%)
    pallas_call x1, Pallas kernels, shards_close(): pl.pallas_call(functools.partial(refine_kernel, (chunks, width, share, si...  55.7 us
    unnamed x4, local copies, waits for them, and re-layouts  2.08 us

profile of v7, /device:TPU:0, one launch (start us, length us, event | category | flops | bytes accessed | tf_op | source)
XLA Modules:
  0.0 58.4 jit_solution(2011944899391088234)
XLA Ops:
  0.6 55.7 %shard_map.77 = (bf16[16,4096]{1,0:T(8,128)(2,1)}, f32[1,128]{1,0:T(1,128)}) custom-call(bf16[128,4096]{1,0:T(8,128)(2,1)} %images.1, s32[1,128]{1,0:T(1,128)} %bitcast.6, s32[1,128]{1,0:T(1,128)} %bitcast.7, bf16[1,128]{1,0:T(2,128)(2,1)} %bitcast.8, f32[16,512]{1,0:T(8,128)} %constant.2.clone.tables, bf16[1,64,4096]{2,1,0:T(8,128)(2,1)} %references.1), custom_call_target="tpu_custom_call" | custom-call | tf_op jit(solution)/shard_map/pallas_call | solution.py:626
  56.3 0.0 copy-start
  56.3 1.6 %copy.10 = bf16[1,16,4096]{2,1,0:T(8,128)(2,1)} copy(bf16[1,16,4096]{2,1,0:T(8,128)(2,1)} %bitcast.5) | data formatting | bytes 262144
  57.9 0.0 copy-done
  57.9 0.5 copy.11
Async XLA Ops:
  56.3 1.6 %copy-start = (f32[1,128]{1,0:T(1,128)S(1)}, f32[1,128]{1,0:T(1,128)}, u32[]{:S(2)}) copy-start(f32[1,128]{1,0:T(1,128)} %get-tuple-element.5) | copy-start | bytes 1540

commit v8 on v7

--- a/solution.py
+++ b/solution.py
@@ -447,7 +447,7 @@
     acc[...] = jnp.zeros_like(acc)
 
     def tick(t, carry):
-        @pl.when(t == 3)
+        @pl.when(t == 4)
         def counts_out():
             s_y_copy.wait_recv()
             total = s_own[...] + sy_got[...].astype(jnp.float32)
@@ -456,9 +456,9 @@
                 sz_send[k - 1] = total[k * share : (k + 1) * share].astype(jnp.bfloat16)
                 s_z_copy(k).start()
 
-        @pl.when((t >= 3) & (t < chunks + 3))
+        @pl.when((t >= 4) & (t < chunks + 4))
         def sum_y():
-            index = t - 3
+            index = t - 4
             y_copy(index).wait_recv()
             total = b_own[index] + y_got[index].astype(jnp.float32)
             z_own[index] = total[:share]
@@ -466,7 +466,7 @@
                 z_send[index, k - 1] = total[k * share : (k + 1) * share].astype(jnp.bfloat16)
                 z_copy(index, k).start()
 
-        @pl.when(t == 5)
+        @pl.when(t == 7)
         def counts_in():
             anchor_copy.wait()
             total = sz_own[...]
@@ -475,9 +475,9 @@
                 total = total + sz_got[k - 1].astype(jnp.float32)
             s_sum[...] = total
 
-        @pl.when((t >= 5) & (t < chunks + 5))
+        @pl.when((t >= 7) & (t < chunks + 7))
         def update():
-            index = t - 5
+            index = t - 7
             total = z_own[index]
             for k in range(1, side_z):
                 z_copy(index, k).wait_recv()
@@ -503,9 +503,9 @@
                 jnp.bfloat16
             )
 
-        @pl.when((t >= 7) & (t < chunks + 7))
+        @pl.when((t >= 10) & (t < chunks + 10))
         def spread():
-            index = t - 7
+            index = t - 10
             for k in range(1, side_z):
                 table_z_copy(index, k).wait_recv()
             table_y_copy(index).start()
@@ -518,9 +518,9 @@
                     crad[t % FAMILIES, span], pick[t], preferred_element_type=jnp.float32
                 ).astype(jnp.bfloat16)
 
-        @pl.when(t >= 9)
+        @pl.when(t >= 13)
         def residuals():
-            index = t - 9
+            index = t - 13
             table_y_copy(index).wait_recv()
             for block in range(4):
                 span = block_rows(block)
@@ -567,7 +567,7 @@
 
         return carry
 
-    lax.fori_loop(0, chunks + 9, tick, 0)
+    lax.fori_loop(0, chunks + 13, tick, 0)
 
     def row_of(family, block):
         part = acc[family, block * LANES : (block + 1) * LANES]

time: 58.6 us -> 61 us (1.041)
  Pallas kernels: 55.7 us -> 58.1 us
    pallas_call x1, Pallas kernels: 55.7 us -> 58.1 us  [shards_close(): pl.pallas_call(functools.partial(refine_kernel, (chunks, width, share, si...]
where the time goes in v8:
time: 61 us; the launch traced here: 60.8 us
  Pallas kernels  58.1 us (95%)
  local copies, waits for them, and re-layouts  2.08 us (3%)
  between operations  0.65 us (1%)
    pallas_call x1, Pallas kernels, shards_close(): pl.pallas_call(functools.partial(refine_kernel, (chunks, width, share, si...  58.1 us
    unnamed x4, local copies, waits for them, and re-layouts  2.08 us

profile of v8, /device:TPU:0, one launch (start us, length us, event | category | flops | bytes accessed | tf_op | source)
XLA Modules:
  0.0 60.8 jit_solution(6614882265534628693)
XLA Ops:
  0.6 58.1 %shard_map.77 = (bf16[16,4096]{1,0:T(8,128)(2,1)}, f32[1,128]{1,0:T(1,128)}) custom-call(bf16[128,4096]{1,0:T(8,128)(2,1)} %images.1, s32[1,128]{1,0:T(1,128)} %bitcast.6, s32[1,128]{1,0:T(1,128)} %bitcast.7, bf16[1,128]{1,0:T(2,128)(2,1)} %bitcast.8, f32[16,512]{1,0:T(8,128)} %constant.2.clone.tables, bf16[1,64,4096]{2,1,0:T(8,128)(2,1)} %references.1), custom_call_target="tpu_custom_call" | custom-call | tf_op jit(solution)/shard_map/pallas_call | solution.py:626
  58.7 0.0 copy-start
  58.7 1.6 %copy.10 = bf16[1,16,4096]{2,1,0:T(8,128)(2,1)} copy(bf16[1,16,4096]{2,1,0:T(8,128)(2,1)} %bitcast.5) | data formatting | bytes 262144
  60.3 0.0 copy-done
  60.3 0.5 copy.11
Async XLA Ops:
  58.7 1.6 %copy-start = (f32[1,128]{1,0:T(1,128)S(1)}, f32[1,128]{1,0:T(1,128)}, u32[]{:S(2)}) copy-start(f32[1,128]{1,0:T(1,128)} %get-tuple-element.5) | copy-start | bytes 1540
